TPU v7x, 32 devices: a whole 2x2x4 slice. The times are simulated.
32 devices in a mesh: dp: 4 (over y, x), head: 8 (over z, core).
Axes of the slice: x: 2, y: 2, z: 4, core: 2. Of those that a mesh axis runs over, the one named last changes fastest.
Arguments:
- block_input: bfloat16 [16384, 1536], P(('dp', 'head')), may hold values from -6 to 6
- lengths: int32 [4, 4], P('dp'), may hold values from 1 to 2048, 4096 in all within a row
- norm_gain: float32 [1536], replicated, may hold values from 0.5 to 1.5
- in_gate: bfloat16 [1536, 3072], P('dp', 'head'), may hold values from -0.15625 to 0.15625
- in_value: bfloat16 [1536, 3072], P('dp', 'head'), may hold values from -0.15625 to 0.15625
- in_states: bfloat16 [1536, 256], P('dp', 'head'), may hold values from -0.15625 to 0.15625
- in_steps: bfloat16 [1536, 48], P('dp', 'head'), may hold values from -0.15625 to 0.15625
- conv_value: float32 [4, 3072], P(None, 'head'), may hold values from -3 to 3
- conv_value_bias: float32 [3072], P('head'), may hold values from -3 to 3
- conv_states: float32 [4, 256], P(None, 'head'), may hold values from -3 to 3
- conv_states_bias: float32 [256], P('head'), may hold values from -3 to 3
- step_bias: float32 [48], P('head'), may hold values from -6 to -2
- decay_log: float32 [48], P('head'), may hold values from 0 to 2.77
- skip_gain: float32 [48], P('head'), may hold values from 0.5 to 1.5
- gate_gain: float32 [3072], P('head'), may hold values from 0.5 to 1.5
- out_proj: bfloat16 [1536, 3072], P('dp', 'head'), may hold values from -0.109375 to 0.109375
- cotangent: bfloat16 [16384, 1536], P(('dp', 'head')), may hold values from -6 to 6
Outputs:
- out: bfloat16 [16384, 1536], P(('dp', 'head'))
- input_grad: bfloat16 [16384, 1536], P(('dp', 'head'))
- grad_norm_gain: float32 [1536], replicated
- grad_in_gate: float32 [1536, 3072], P('dp', 'head')
- grad_in_value: float32 [1536, 3072], P('dp', 'head')
- grad_in_states: float32 [1536, 256], P('dp', 'head')
- grad_in_steps: float32 [1536, 48], P('dp', 'head')
- grad_conv_value: float32 [4, 3072], P(None, 'head')
- grad_conv_value_bias: float32 [3072], P('head')
- grad_conv_states: float32 [4, 256], P(None, 'head')
- grad_conv_states_bias: float32 [256], P('head')
- grad_step_bias: float32 [48], P('head')
- grad_decay_log: float32 [48], P('head')
- grad_skip_gain: float32 [48], P('head')
- grad_gate_gain: float32 [3072], P('head')
- grad_out_proj: float32 [1536, 3072], P('dp', 'head')
Inputs may be any that keep to these rules, and one draw needn't show every extreme that they name: Each row holds, in order, the lengths of the 4 sequences packed into one group of 4096 tokens; a row sums to 4096, and its longest sequence has exactly half of 4096 tokens.
All inputs are finite; a program needn't handle non-finite values.
Results may differ from a plain program's by a relative error of at most 0.012.
Values may be sent and summed in bfloat16 or wider, within the bound.
A program may use at most 320 MiB of HBM per device.

v0:
```python
import jax
import jax.numpy as jnp
from jax import lax
from jax.sharding import PartitionSpec as P

SPAN = 256


EPSILON = 1e-05
HIGHEST = lax.Precision.HIGHEST


def segment_numbers(lengths, count):
    ends = jnp.cumsum(lengths, axis=1)
    places = jnp.arange(count, dtype=jnp.int32)
    return jnp.sum((places[None, :, None] >= ends[:, None, :]).astype(jnp.int32), axis=2)


def causal_conv(source, weight, offset_bias, segment):
    tap_count = weight.shape[0]
    length = source.shape[0]
    running = offset_bias[None, :] + weight[tap_count - 1][None, :] * source
    for offset in range(1, tap_count):
        shifted = jnp.pad(source, ((offset, 0), (0, 0)))[:length]
        earlier = jnp.pad(segment, (offset, 0), constant_values=-1)[:length]
        matching = (earlier == segment).astype(jnp.float32)
        running = running + weight[tap_count - 1 - offset][None, :] * shifted * matching[:, None]
    return jax.nn.silu(running)


def state_space(values, steps, rates, keys_in, query_in, segment, block):
    count = values.shape[0] // block
    heads = values.shape[1]
    width = values.shape[2]
    pieces = (
        values.reshape(count, block, heads, width),
        steps.reshape(count, block, heads),
        keys_in.reshape(count, block, -1),
        query_in.reshape(count, block, -1),
        segment.reshape(count, block),
    )
    lower_mask = jnp.tril(jnp.ones((block, block), dtype=bool))

    def advance(carry, piece):
        state, previous = carry
        value_block, step_block, keys_block, query_block, seg_block = piece
        decays = jnp.cumsum(step_block * rates[None, :], axis=0)
        within = lower_mask & (seg_block[:, None] == seg_block[None, :])
        spread = decays[:, None, :] - decays[None, :, :]
        weights = jnp.exp(jnp.where(within[:, :, None], spread, -1e30))
        scores = jnp.dot(query_block, keys_block.T, precision=HIGHEST)
        driven = value_block * step_block[:, :, None]
        inside = jnp.einsum("tsh,shp->thp", scores[:, :, None] * weights, driven, precision=HIGHEST)
        carried = (seg_block == previous).astype(jnp.float32)
        reach = jnp.exp(decays) * carried[:, None]
        outside = (
            jnp.einsum("tn,hpn->thp", query_block, state, precision=HIGHEST) * reach[:, :, None]
        )
        final = seg_block[-1]
        kept = (final == previous).astype(jnp.float32)
        tail = (
            jnp.exp(decays[-1][None, :] - decays)
            * (seg_block == final).astype(jnp.float32)[:, None]
        )
        fresh = jnp.einsum("sh,shp,sn->hpn", tail, driven, keys_block, precision=HIGHEST)
        state = state * (jnp.exp(decays[-1]) * kept)[:, None, None] + fresh
        return ((state, final), inside + outside)

    start = (
        jnp.zeros((heads, width, keys_in.shape[1]), jnp.float32),
        jnp.array(-1, dtype=jnp.int32),
    )
    _, result = lax.scan(jax.checkpoint(advance), start, pieces)
    return result.reshape(values.shape)


def mixer(values, states, gate_pre, steps_pre, step_bias, decay_log, skip_gain, segment):
    heads = step_bias.shape[0]
    state_width = states.shape[1] // 2
    steps = jax.nn.softplus(steps_pre + step_bias[None, :])
    rates = -jnp.exp(decay_log)
    shaped = values.reshape(values.shape[0], heads, -1)
    result = state_space(
        shaped, steps, rates, states[:, :state_width], states[:, state_width:], segment, SPAN
    )
    result = result + skip_gain[None, :, None] * shaped
    return result.reshape(values.shape) * jax.nn.silu(gate_pre)


def times_transpose(left, matrix):
    return lax.dot_general(
        left, matrix, (((1,), (1,)), ((), ())), preferred_element_type=jnp.float32
    )


def over_tokens(left, right):
    return lax.dot_general(
        left, right, (((0,), (0,)), ((), ())), preferred_element_type=jnp.float32
    )


def shards(
    block_input,
    lengths,
    norm_gain,
    in_gate,
    in_value,
    in_states,
    in_steps,
    conv_value,
    conv_value_bias,
    conv_states,
    conv_states_bias,
    step_bias,
    decay_log,
    skip_gain,
    gate_gain,
    out_proj,
    cotangent,
):
    gathered = lax.all_gather(block_input, "head", axis=0, tiled=True)
    gate_matrix, value_matrix, states_matrix, steps_matrix, out_matrix = (
        lax.all_gather(in_gate, "dp", axis=0, tiled=True),
        lax.all_gather(in_value, "dp", axis=0, tiled=True),
        lax.all_gather(in_states, "dp", axis=0, tiled=True),
        lax.all_gather(in_steps, "dp", axis=0, tiled=True),
        lax.all_gather(out_proj, "dp", axis=0, tiled=True),
    )
    segment = segment_numbers(lengths, gathered.shape[0])[0]
    own_count = block_input.shape[0]
    own_start = lax.axis_index("head") * own_count
    rows = gathered.astype(jnp.float32)
    inverse = lax.rsqrt(jnp.mean(rows * rows, axis=1, keepdims=True) + EPSILON)
    scaled = rows * inverse
    normed = (scaled * norm_gain[None, :]).astype(jnp.bfloat16)
    gate_pre = jnp.dot(normed, gate_matrix, preferred_element_type=jnp.float32)
    value_pre = jnp.dot(normed, value_matrix, preferred_element_type=jnp.float32)
    states_pre = jnp.dot(normed, states_matrix, preferred_element_type=jnp.float32)
    steps_pre = jnp.dot(normed, steps_matrix, preferred_element_type=jnp.float32)

    def convolve(source, weight, offset_bias):
        return causal_conv(source, weight, offset_bias, segment)

    states_own, states_pull = jax.vjp(convolve, states_pre, conv_states, conv_states_bias)
    states_full = lax.all_gather(
        states_own.astype(jnp.bfloat16), "head", axis=1, tiled=True
    ).astype(jnp.float32)
    value_conv, value_pull = jax.vjp(convolve, value_pre, conv_value, conv_value_bias)
    values = lax.optimization_barrier(value_conv.astype(jnp.bfloat16)).astype(jnp.float32)

    def local_mixer(values, states, gate_pre, steps_pre, step_bias, decay_log, skip_gain):
        return mixer(values, states, gate_pre, steps_pre, step_bias, decay_log, skip_gain, segment)

    mixed, mixer_pull = jax.vjp(
        local_mixer, values, states_full, gate_pre, steps_pre, step_bias, decay_log, skip_gain
    )
    total_width = mixed.shape[1] * lax.axis_size("head")
    squares = lax.psum(jnp.sum(mixed * mixed, axis=1, keepdims=True), "head")
    inverse_gate = lax.rsqrt(squares / total_width + EPSILON)
    gated = (mixed * gate_gain[None, :]).astype(jnp.bfloat16)
    partial_branch = times_transpose(gated, out_matrix)
    branch = lax.psum_scatter(partial_branch, "head", scatter_dimension=0, tiled=True)
    own_rows = block_input.astype(jnp.float32)
    own_inverse_gate = lax.dynamic_slice_in_dim(inverse_gate, own_start, own_count, 0)
    result = (own_rows + own_inverse_gate * branch).astype(jnp.bfloat16)
    grad_rows = lax.all_gather(cotangent, "head", axis=0, tiled=True)
    upstream = cotangent.astype(jnp.float32)
    grad_float = grad_rows.astype(jnp.float32)
    gate_dots = lax.psum(jnp.sum(grad_float * partial_branch, axis=1, keepdims=True), "head")
    branch_grad = (inverse_gate * grad_float).astype(jnp.bfloat16)
    gated_grad = jnp.dot(branch_grad, out_matrix, preferred_element_type=jnp.float32)
    grad_out = over_tokens(branch_grad, gated)
    cubed = inverse_gate * inverse_gate * inverse_gate
    mixed_grad = gated_grad * gate_gain[None, :] - gate_dots * cubed / total_width * mixed
    grad_gate = jnp.sum(gated_grad * mixed, axis=0)
    values_grad, states_grad, gate_grad, steps_grad, grad_step, grad_decay, grad_skip = mixer_pull(
        mixed_grad
    )
    states_own_grad = lax.psum_scatter(states_grad, "head", scatter_dimension=1, tiled=True)
    value_pre_grad, grad_conv_value, grad_value_bias = value_pull(values_grad)
    states_pre_grad, grad_conv_states, grad_states_bias = states_pull(states_own_grad)
    gate_low = gate_grad.astype(jnp.bfloat16)
    value_low = value_pre_grad.astype(jnp.bfloat16)
    states_low = states_pre_grad.astype(jnp.bfloat16)
    steps_low = steps_grad.astype(jnp.bfloat16)
    normed_grad = (
        times_transpose(gate_low, gate_matrix)
        + times_transpose(value_low, value_matrix)
        + times_transpose(states_low, states_matrix)
        + times_transpose(steps_low, steps_matrix)
    )
    grad_gate_matrix = over_tokens(normed, gate_low)
    grad_value_matrix = over_tokens(normed, value_low)
    grad_states_matrix = over_tokens(normed, states_low)
    grad_steps_matrix = over_tokens(normed, steps_low)
    feature_count = rows.shape[1]
    full_grad = lax.psum(normed_grad, "head")
    gain_grad = full_grad * norm_gain[None, :]
    row_dots = jnp.sum(gain_grad * rows, axis=1, keepdims=True)
    rows_grad = (
        inverse * gain_grad - rows * (inverse * inverse * inverse / feature_count) * row_dots
    )
    own_grad = lax.dynamic_slice_in_dim(rows_grad, own_start, own_count, 0)
    grad_norm = jnp.sum(full_grad * scaled, axis=0)
    input_grad = (upstream + own_grad).astype(jnp.bfloat16)
    sum_gate, sum_value, sum_states, sum_steps, sum_out = (
        lax.psum_scatter(grad_gate_matrix, "dp", scatter_dimension=0, tiled=True),
        lax.psum_scatter(grad_value_matrix, "dp", scatter_dimension=0, tiled=True),
        lax.psum_scatter(grad_states_matrix, "dp", scatter_dimension=0, tiled=True),
        lax.psum_scatter(grad_steps_matrix, "dp", scatter_dimension=0, tiled=True),
        lax.psum_scatter(grad_out, "dp", scatter_dimension=0, tiled=True),
    )
    (
        tot_norm,
        tot_conv_value,
        tot_value_bias,
        tot_conv_states,
        tot_states_bias,
        tot_step,
        tot_decay,
        tot_skip,
        tot_gate,
    ) = lax.psum(
        (
            grad_norm,
            grad_conv_value,
            grad_value_bias,
            grad_conv_states,
            grad_states_bias,
            grad_step,
            grad_decay,
            grad_skip,
            grad_gate,
        ),
        "dp",
    )
    return (
        result,
        input_grad,
        tot_norm,
        sum_gate,
        sum_value,
        sum_states,
        sum_steps,
        tot_conv_value,
        tot_value_bias,
        tot_conv_states,
        tot_states_bias,
        tot_step,
        tot_decay,
        tot_skip,
        tot_gate,
        sum_out,
    )


def solution(mesh):
    return jax.shard_map(
        shards,
        mesh=mesh,
        in_specs=(
            P(("dp", "head"), None),
            P("dp", None),
            P(),
            P("dp", "head"),
            P("dp", "head"),
            P("dp", "head"),
            P("dp", "head"),
            P(None, "head"),
            P("head"),
            P(None, "head"),
            P("head"),
            P("head"),
            P("head"),
            P("head"),
            P("head"),
            P("dp", "head"),
            P(("dp", "head"), None),
        ),
        out_specs=(
            P(("dp", "head"), None),
            P(("dp", "head"), None),
            P(),
            P("dp", "head"),
            P("dp", "head"),
            P("dp", "head"),
            P("dp", "head"),
            P(None, "head"),
            P("head"),
            P(None, "head"),
            P("head"),
            P("head"),
            P("head"),
            P("head"),
            P("head"),
            P("dp", "head"),
        ),
        check_vma=False,
    )
```

profile of v0, /device:TPU:0, one launch (start us, length us, event | category | flops | bytes accessed | tf_op | source)
XLA Modules:
  0.0 2444.1 jit_solution(11867225004580377628)
XLA Ops:
  9.8 10.1 all_gather.27
  20.7 108.4 %all-gather.7.cloned.1.call-done = bf16[4096,1536]{1,0:T(8,128)(2,1)} async-done(((bf16[512,1536]{1,0:T(8,128)(2,1)}), bf16[4096,1536]{1,0:T(8,128)(2,1)}) %all-gather.7.cloned.1.call-update) | async-done | bytes 12582928 | tf_op jit(solution)/shard_map/all_gather | solution.py:121
  165.9 10.1 fusion.153
  215.5 399.6 %while.45 = (s32[]{:T(128)}, f32[6,64,128]{2,1,0:T(8,128)S(1)}, s32[]{:T(128)}, f32[16,256,6,64]{1,0,3,2:T(8,128)}, f32[16,6,64,128]{3,2,1,0:T(8,128)}, /*index=...) while((s32[]{:T(128)}, f32[6,64,128]{2,1,0:T(8,128)S(1)}, ...), condition=%wide.region_6.7_spmd.clone, body=%wide.region_3.6_spmd.clone.sunk | while | flops 706960384 | bytes 5842398 | solution.py:73
  229.8 9.9 dynamic_update_slice.75
  254.8 10.1 dynamic_update_slice.75
  280.0 9.9 dynamic_update_slice.75
  615.1 11.3 copy.316
  633.2 15.2 multiply_reduce_fusion.12
  648.4 15.8 fusion.97
  664.2 26.0 %all-reduce.27 = (f32[4096,1]{0,1:T(1,128)S(1)}, f32[4096,1]{0,1:T(1,128)S(1)}) all-reduce(f32[4096,1]{0,1:T(1,128)S(1)} %bitcast.442, f32[4096,1]{0,1:T(1,128)S(1)} %bitcast.438), channel_id=1, replica_groups=mesh['dp'=4,'head'=8] {'head'}, use_global_device_ids=true, to_apply=%region_8.9 | all-reduce | flops 8192 | bytes 65536 | tf_op jit(solution)/shard_map/psum | solution.py:158
  690.2 22.4 multiply_reduce_fusion.7
  733.9 665.4 %while.46 = (s32[]{:T(128)}, f32[6]{0:T(128)S(1)}, f32[6,64,128]{2,1,0:T(8,128)S(1)}, f32[16,256,6,64]{1,0,3,2:T(8,128)}, f32[16,256,6]{1,2,0:T(8,128)S(1)}, /*i...) while((s32[]{:T(128)}, f32[6]{0:T(128)S(1)}, ...), condition=%wide.region_25.26_spmd.clone, body=%wide.region_12.25_spmd.clone.sunk | while | flops 1668003328 | bytes 15057286 | solution.py:73
  1408.4 11.3 copy.318
  1427.1 18.3 multiply_reduce_fusion.11
  1450.8 13.6 fusion.155
  1464.4 11.9 fusion.156
  1479.8 10.4 fusion.157
  1490.1 33.3 %add_add_fusion = f32[4096,1536]{1,0:T(8,128)} fusion(f32[4096,1536]{1,0:T(8,128)} %fusion.157, f32[4096,1536]{1,0:T(8,128)} %fusion.155, f32[4096,1536]{1,0:T(8,128)} %fusion.156, bf16[1536,6]{0,1:T(8,128)(2,1)S(1)} %copy-done.22, bf16[4096,6]{0,1:T(8,128)(2,1)S(1)} %get-tuple-element.989), kind=kOutput, calls=%fused_computation.146 | convolution fusion | flops 94371840 | bytes 100730880 | tf_op jit(solution)/shard_map/dot_general | solution.py:91
  1532.4 11.9 fusion.158
  1544.4 10.9 fusion.159
  1555.4 12.7 fusion.98
  1570.0 14.9 convert_element_type.137
  1592.8 418.7 %all-reduce.31.cloned.1.call-done = f32[4096,1536]{1,0:T(8,128)} async-done(((f32[4096,1536]{1,0:T(8,128)}), f32[4096,1536]{1,0:T(8,128)}) %all-reduce.31.cloned.1.call-update) | async-done | bytes 25165840 | tf_op jit(solution)/shard_map/psum | solution.py:197
  2011.4 16.2 multiply_reduce_fusion.3
  2031.6 16.5 all-reduce.28
  2048.2 213.0 %reduce-scatter.8.cloned.1.call-done = f32[512,1536]{0,1:T(8,128)} async-done(((f32[4096,1536]{0,1:T(8,128)}), f32[512,1536]{0,1:T(8,128)}) %reduce-scatter.8.cloned.1.call-update) | async-done | bytes 3145744 | tf_op jit(solution)/shard_map/reduce_scatter | solution.py:162
  2265.2 20.6 reduce-scatter.18.cloned.1.call-done
  2285.8 41.4 %reduce-scatter.12.cloned.1.call-done = f32[384,384]{1,0:T(8,128)} async-done(((f32[1536,384]{1,0:T(8,128)}), f32[384,384]{1,0:T(8,128)}) %reduce-scatter.12.cloned.1.call-update) | async-done | bytes 589840 | tf_op jit(solution)/shard_map/reduce_scatter | solution.py:207
  2327.2 41.2 %reduce-scatter.14.cloned.1.call-done = f32[384,384]{1,0:T(8,128)} async-done(((f32[1536,384]{1,0:T(8,128)}), f32[384,384]{1,0:T(8,128)}) %reduce-scatter.14.cloned.1.call-update) | async-done | bytes 589840 | tf_op jit(solution)/shard_map/reduce_scatter | solution.py:208
  2368.3 41.3 %reduce-scatter.20.cloned.1.call-done = f32[384,384]{1,0:T(8,128)} async-done(((f32[1536,384]{1,0:T(8,128)}), f32[384,384]{1,0:T(8,128)}) %reduce-scatter.20.cloned.1.call-update) | async-done | bytes 589840 | tf_op jit(solution)/shard_map/reduce_scatter | solution.py:211
  2409.7 27.4 %reduce-scatter.16.cloned.1.call-done = f32[384,32]{0,1:T(8,128)} async-done(((f32[1536,32]{0,1:T(8,128)}), f32[384,32]{0,1:T(8,128)}) %reduce-scatter.16.cloned.1.call-update) | async-done | bytes 49168 | tf_op jit(solution)/shard_map/reduce_scatter | solution.py:209
  (1485 shorter events, 1148.6 us)
Async XLA Ops:
  7.2 121.9 %all-gather.7.cloned.1.call-start = ((), (), s32[]{:S(2)}) async-start(), calls=%async_computation.7 | async-start | bytes 14155776 | tf_op jit(solution)/shard_map/all_gather | solution.py:121
  7.9 158.0 %all-gather.9.cloned.1.call-start = ((), (), s32[]{:S(2)}) async-start(), calls=%async_computation.8 | async-start | bytes 1474560 | tf_op jit(solution)/shard_map/all_gather | solution.py:124
  8.7 194.8 %all-gather.11.cloned.1.call-start = ((), (), s32[]{:S(2)}) async-start(), calls=%async_computation.9 | async-start | bytes 2359296 | tf_op jit(solution)/shard_map/all_gather | solution.py:145
  9.7 139.8 %copy-start.14 = (f32[4096]{0:T(1024)}, f32[4096]{0:T(1024)S(1)}, u32[]{:S(2)}) copy-start(f32[4096]{0:T(1024)S(1)} %get-tuple-element.1029) | copy-start | bytes 49156
  9.8 139.8 %copy-start.17 = (f32[4096]{0:T(1024)}, f32[4096]{0:T(1024)S(1)}, u32[]{:S(2)}) copy-start(f32[4096]{0:T(1024)S(1)} %get-tuple-element.1030) | copy-start | bytes 49156
  9.8 166.3 %copy-start.12 = (f32[4096]{0:T(1024)}, f32[4096]{0:T(1024)S(1)}, u32[]{:S(2)}) copy-start(f32[4096]{0:T(1024)S(1)} %get-tuple-element.1028) | copy-start | bytes 49156
  19.9 124.7 %copy-start.10 = (bf16[1536,32]{0,1:T(8,128)(2,1)}, bf16[1536,32]{0,1:T(8,128)(2,1)S(1)}, u32[]{:S(2)}) copy-start(bf16[1536,32]{0,1:T(8,128)(2,1)S(1)} %all_gather.27) | copy-start | bytes 294916
  20.7 128.9 %copy-start.48 = (f32[32]{0:T(128)}, f32[32]{0:T(128)S(1)}, u32[]{:S(2)}) copy-start(f32[32]{0:T(128)S(1)} %get-tuple-element.1031) | copy-start | bytes 388
  20.7 128.9 %copy-start.50 = (f32[32]{0:T(128)}, f32[32]{0:T(128)S(1)}, u32[]{:S(2)}) copy-start(f32[32]{0:T(128)S(1)} %get-tuple-element.1032) | copy-start | bytes 388
  20.7 128.9 %copy-start.52 = (f32[32]{0:T(128)}, f32[32]{0:T(128)S(1)}, u32[]{:S(2)}) copy-start(f32[32]{0:T(128)S(1)} %get-tuple-element.1033) | copy-start | bytes 388
  20.7 128.9 %copy-start.54 = (f32[32]{0:T(128)}, f32[32]{0:T(128)S(1)}, u32[]{:S(2)}) copy-start(f32[32]{0:T(128)S(1)} %get-tuple-element.1034) | copy-start | bytes 388
  20.7 116.1 %copy-start.26 = (f32[1536]{0:T(1024)S(1)}, f32[1536]{0:T(1024)}, u32[]{:S(2)}) copy-start(f32[1536]{0:T(1024)} %param.23) | copy-start | bytes 18436
  149.5 15.6 copy-start.62
  151.7 481.4 %all-gather.13.cloned.1.call-start = ((), (), s32[]{:S(2)}) async-start(), calls=%async_computation.10 | async-start | bytes 1474560 | tf_op jit(solution)/shard_map/all_gather | solution.py:123
  152.3 496.1 %all-gather.15.cloned.1.call-start = ((), (), s32[]{:S(2)}) async-start(), calls=%async_computation.11 | async-start | bytes 1474560 | tf_op jit(solution)/shard_map/all_gather | solution.py:127
  152.9 495.5 %all-gather.17.cloned.1.call-start = ((), (), s32[]{:S(2)}) async-start(), calls=%async_computation.13 | async-start | bytes 14155776 | tf_op jit(solution)/shard_map/all_gather | solution.py:166
  154.5 1321.7 %reduce-scatter.10.cloned.1.call-start = ((), (), s32[]{:S(2)}) async-start(), calls=%async_computation.14 | async-start | bytes 4718592 | tf_op jit(solution)/shard_map/reduce_scatter | solution.py:179
  633.2 15.2 copy-start.42
  690.2 22.4 copy-start.28
  1408.1 603.3 %all-reduce.31.cloned.1.call-start = ((), (), s32[]{:S(2)}) async-start(), calls=%async_computation.15 | async-start | bytes 50331648 | tf_op jit(solution)/shard_map/psum | solution.py:197
  1427.1 18.3 copy-start.33
  1427.1 18.3 copy-start.35
  1427.1 18.3 copy-start.37
  1523.4 737.8 %reduce-scatter.8.cloned.1.call-start = ((), (), s32[]{:S(2)}) async-start(), calls=%async_computation.12 | async-start | bytes 28311552 | tf_op jit(solution)/shard_map/reduce_scatter | solution.py:162
  1524.2 761.6 %reduce-scatter.18.cloned.1.call-start = ((), (), s32[]{:S(2)}) async-start(), calls=%async_computation.19 | async-start | bytes 61440 | tf_op jit(solution)/shard_map/reduce_scatter | solution.py:210
  1532.3 794.8 %reduce-scatter.12.cloned.1.call-start = ((), (), s32[]{:S(2)}) async-start(), calls=%async_computation.16 | async-start | bytes 2949120 | tf_op jit(solution)/shard_map/reduce_scatter | solution.py:207
  1544.3 824.0 %reduce-scatter.14.cloned.1.call-start = ((), (), s32[]{:S(2)}) async-start(), calls=%async_computation.17 | async-start | bytes 2949120 | tf_op jit(solution)/shard_map/reduce_scatter | solution.py:208
  1555.3 854.4 %reduce-scatter.20.cloned.1.call-start = ((), (), s32[]{:S(2)}) async-start(), calls=%async_computation.20 | async-start | bytes 2949120 | tf_op jit(solution)/shard_map/reduce_scatter | solution.py:211
  1568.1 869.0 %reduce-scatter.16.cloned.1.call-start = ((), (), s32[]{:S(2)}) async-start(), calls=%async_computation.18 | async-start | bytes 245760 | tf_op jit(solution)/shard_map/reduce_scatter | solution.py:209
  1570.0 15.2 copy-start.64
  1585.1 426.3 %copy-start.27 = (f32[1536]{0:T(1024)S(1)}, f32[1536]{0:T(1024)}, u32[]{:S(2)}) copy-start(f32[1536]{0:T(1024)} %param.23) | copy-start | bytes 18436
  1592.7 435.0 %copy-start.7 = (bf16[512,1536]{1,0:T(8,128)(2,1)S(1)}, bf16[512,1536]{1,0:T(8,128)(2,1)}, u32[]{:S(2)}) copy-start(bf16[512,1536]{1,0:T(8,128)(2,1)} %param.37) | copy-start | bytes 4718596
  (51 other events, 468.1 us)
Sparse Core Ops, SparseCore 0:
  9.7 119.4 all-gather.6
  131.0 25.9 all-gather.8
  159.1 29.0 all-gather.10
  190.0 27.2 all-gather.12
  218.9 27.7 all-gather.14
  248.7 116.7 all-gather.16
  1408.3 47.3 reduce-scatter.9
  1523.5 487.8 all-reduce.30
  2013.8 247.3 reduce-scatter.7
  2264.3 21.4 reduce-scatter.17
  2289.7 37.3 reduce-scatter.11
  2330.9 37.3 reduce-scatter.13
  2372.2 37.3 reduce-scatter.19
  2413.1 23.9 reduce-scatter.15
where the time goes:
time: 2460 us; the launch traced here: 2440 us
  waiting for transfers between devices  915 us (37%)
  local copies, waits for them, and re-layouts  606 us (25%)
  matrix products  456 us (19%)
  other arithmetic  344 us (14%)
  blocking collectives  61.3 us (2%)
  loops' own time  45.7 us (2%)
    psum x1, waiting for transfers between devices, shards(): full_grad = lax.psum(normed_grad, 'head')  419 us
    dynamic_update_slice x80, local copies, waits for them, and re-layouts, state_space(): _, result = lax.scan(jax.checkpoint(advance), start, pieces)  331 us
    reduce_scatter x1, waiting for transfers between devices, shards(): lax.psum_scatter(partial_branch, 'head', scatter_dimension=0, tiled=True)  213 us
    another operation x129, other arithmetic  183 us
    all_gather x1, waiting for transfers between devices, shards(): gathered = lax.all_gather(block_input, 'head', axis=0, tiled=True)  108 us
    dot_general x48, matrix products, advance(): jnp.einsum('tsh,shp->thp', scores[:, :, None] * weights, driven, precisio...  104 us
    dot_general x5, matrix products, times_transpose(): lax.dot_general(left, matrix, (((1,), (1,)), ((), ())), preferred_element...  84.9 us
    dynamic_slice x64, local copies, waits for them, and re-layouts, state_space(): _, result = lax.scan(jax.checkpoint(advance), start, pieces)  66.6 us
  transfers between devices with their start and end apart: 14, of which 8 were waited for; matrix products, arithmetic and copies ran while one was open for 26% of the time, Pallas kernels for 0%

commit v1 on v0

v1 whole, which is shorter than its diff:
```python
import functools

import jax
import jax.numpy as jnp
from jax import lax
from jax.experimental import pallas as pl
from jax.experimental.pallas import tpu as pltpu
from jax.sharding import PartitionSpec as P

EPSILON = 1e-05
HALO = 16
LH = 128
QB = 128
LOG2E = 1.4426950408889634
TINY = 1e-30
F32 = jnp.float32
BF16 = jnp.bfloat16
MESH = pl.DeviceIdType.MESH
MIB = 1024 * 1024


def mm(a, b, ca, cb):
    return lax.dot_general(a, b, (((ca,), (cb,)), ((), ())), preferred_element_type=F32)


def shape(dims, dtype):
    return jax.ShapeDtypeStruct(dims, dtype)


def params(limit=48):
    return pltpu.CompilerParams(vmem_limit_bytes=limit * MIB)


def cost(flops, nbytes):
    return pl.CostEstimate(flops=int(flops), transcendentals=0, bytes_accessed=int(nbytes))


def chunk_of(count, most, unit):
    best = unit
    for size in range(unit, most + 1, unit):
        if count % size == 0:
            best = size
    return best


def sigmoid(v):
    return 0.5 * jnp.tanh(0.5 * v) + 0.5


def lane_chunks(count, most=256):
    return [pl.ds(base, most) for base in range(0, count, most)]


def folded(v):
    out = v[:, 0:128]
    for base in range(128, v.shape[1], 128):
        out = out + v[:, base : base + 128]
    return out


def lane_cumsum(v, reverse=False):
    size = v.shape[1]
    lane = lax.broadcasted_iota(jnp.int32, v.shape, 1)
    step = 1
    while step < size:
        if reverse:
            moved = pltpu.roll(v, size - step, 1)
            v = v + jnp.where(lane < size - step, moved, 0.0)
        else:
            moved = pltpu.roll(v, step, 1)
            v = v + jnp.where(lane >= step, moved, 0.0)
        step *= 2
    return v


def block_terms(dt, a2, seg_ref, b):
    cum = lane_cumsum(a2)
    logdt = jnp.log2(jnp.maximum(dt, TINY))
    source = cum - logdt
    q = dt.shape[1]
    prev = seg_ref[0:1, pl.ds(pl.multiple_of(b * q, q), q)][:, q - 1 :]
    segr = seg_ref[0:1, pl.ds(pl.multiple_of(LH + b * q, q), q)]
    segc = jnp.broadcast_to(segr, (q, q)).T
    last = cum[:, q - 1 : q]
    final = segr[:, q - 1 : q]
    reach = jnp.where(segr == prev, jnp.exp2(cum), 0.0)
    tail = jnp.where(segr == final, jnp.exp2(last - source), 0.0)
    kept = jnp.where(final == prev, jnp.exp2(last), 0.0)
    pad = (-dt.shape[0]) % 128
    padded = jnp.concatenate([source, jnp.zeros((pad, q), F32)], axis=0) if pad else source
    columns = padded.T
    row_s = lax.broadcasted_iota(jnp.int32, (q, q), 0)
    col_t = lax.broadcasted_iota(jnp.int32, (q, q), 1)
    bias = jnp.where((row_s <= col_t) & (segc == segr), 0.0, -1e30)
    return cum, columns, reach, tail, kept, bias


def scan_fwd_kernel(
    places, width,
    x_ref, dt_ref, a_ref, seg_ref, b_ref, c_ref, sin_ref, skip_ref,
    y_ref, st_ref, state,
):
    @pl.when(pl.program_id(0) == 0)
    def _():
        state[...] = sin_ref[...].astype(F32)

    cum, columns, reach, tail, kept, bias = block_terms(dt_ref[...], a_ref[...], seg_ref, pl.program_id(0))
    gt = mm(b_ref[...], c_ref[...], 1, 1)
    low = state[...].astype(BF16)
    st_ref[0] = low
    y_ref[...] = mm(low, c_ref[...], 1, 1)
    for i, h in enumerate(places):
        rows = slice(i * width, (i + 1) * width)
        weights = jnp.exp2(cum[h : h + 1] - columns[:, h : h + 1] + bias)
        mix = (gt * weights).astype(BF16)
        xh = x_ref[rows]
        xf = xh.astype(F32)
        y_ref[rows] = mm(xh, mix, 1, 0) + y_ref[rows] * reach[h : h + 1] + skip_ref[h, 0] * xf
        xs = (xf * tail[h : h + 1]).astype(BF16)
        state[rows] = state[rows] * kept[h : h + 1] + mm(xs, b_ref[...], 1, 0)


def scan_bwd_kernel(
    places, width,
    x_ref, dy_ref, y_ref, dt_ref, a_ref, seg_ref, b_ref, c_ref,
    st_ref, rin_ref, skip_ref,
    dx_ref, db_ref, dc_ref, xdx_ref, da_ref,
    adjoint, xs_all, ds_all, rows_v, rows_c, rows_r, rows_e,
):
    @pl.when(pl.program_id(0) == 0)
    def _():
        adjoint[...] = rin_ref[...].astype(F32)

    cum, columns, reach, tail, kept, bias = block_terms(
        dt_ref[...], a_ref[...], seg_ref, pl.num_programs(0) - 1 - pl.program_id(0)
    )
    bk, ck = b_ref[...], c_ref[...]
    gt = mm(bk, ck, 1, 1)
    r_low = adjoint[...].astype(BF16)
    s_low = st_ref[0]
    dx_ref[...] = mm(r_low, bk, 1, 1)
    dg = jnp.zeros(gt.shape, F32)
    for i, h in enumerate(places):
        rows = slice(i * width, (i + 1) * width)
        weights = jnp.exp2(cum[h : h + 1] - columns[:, h : h + 1] + bias)
        mix = (gt * weights).astype(BF16)
        xh, dyh = x_ref[rows], dy_ref[rows]
        xf, dyf = xh.astype(F32), dyh.astype(F32)
        pairs = mm(xh, dyh, 0, 0)
        dg = dg + weights * pairs
        inner = mm(dyh, mix, 1, 1)
        outer = dx_ref[rows] * tail[h : h + 1]
        skip = skip_ref[h, 0]
        rows_v[h : h + 1] = jnp.sum(xf * outer, axis=0, keepdims=True)
        rows_c[h : h + 1] = jnp.sum(xf * inner, axis=0, keepdims=True)
        rows_r[h : h + 1] = jnp.sum(dyf * (y_ref[rows] - skip * xf), axis=0, keepdims=True)
        dx_ref[rows] = inner + outer + skip * dyf
        xs_all[rows] = (xf * tail[h : h + 1]).astype(BF16)
        ds = (dyf * reach[h : h + 1]).astype(BF16)
        ds_all[rows] = ds
        carried = adjoint[rows] * kept[h : h + 1]
        rows_e[h : h + 1] = jnp.sum(carried * s_low[rows].astype(F32), axis=0, keepdims=True)
        adjoint[rows] = carried + mm(ds, ck, 1, 0)
    dgl = dg.astype(BF16)
    db_ref[...] = mm(xs_all[...], r_low, 0, 0) + mm(dgl, ck, 1, 0)
    dc_ref[...] = mm(ds_all[...], s_low, 0, 0) + mm(dgl, bk, 0, 0)
    v, c = rows_v[...], rows_c[...]
    xdx_ref[...] = v + c
    ends = jnp.sum(rows_e[...], axis=1, keepdims=True)
    da_ref[...] = lane_cumsum(rows_r[...] - c, True) + (lane_cumsum(v) - v) + ends


def scan_specs(inner, heads, state, nb, flip):
    def at(b):
        return nb - 1 - b if flip else b

    lanes = pl.BlockSpec((inner, QB), lambda b: (0, at(b)))
    per_head = pl.BlockSpec((heads, QB), lambda b: (0, at(b)))
    seg = pl.BlockSpec((8, LH + nb * QB), lambda b: (0, 0))
    nat = pl.BlockSpec((QB, state), lambda b: (at(b), 0))
    full = pl.BlockSpec((inner, state), lambda b: (0, 0))
    skip = pl.BlockSpec(memory_space=pltpu.SMEM)
    st = pl.BlockSpec((1, inner, state), lambda b: (at(b), 0, 0))
    return lanes, per_head, seg, nat, full, skip, st


def scan_forward(places, x, dt, a2, seg, bm, cm, sin, skip):
    heads, tokens = dt.shape
    inner, state = x.shape[0], bm.shape[1]
    nb = tokens // QB
    lanes, per_head, sg, nat, full, sk, st = scan_specs(inner, heads, state, nb, False)
    return pl.pallas_call(
        functools.partial(scan_fwd_kernel, places, inner // len(places)),
        grid=(nb,),
        in_specs=[lanes, per_head, per_head, sg, nat, nat, full, sk],
        out_specs=[lanes, st],
        out_shape=[
            jax.ShapeDtypeStruct((inner, tokens), F32),
            jax.ShapeDtypeStruct((nb, inner, state), BF16),
        ],
        scratch_shapes=[pltpu.VMEM((inner, state), F32)],
        compiler_params=params(),
        cost_estimate=pl.CostEstimate(
            flops=20 * inner * tokens * state, transcendentals=0, bytes_accessed=10 * x.size
        ),
    )(x, dt, a2, seg, bm, cm, sin, skip)


def scan_backward(places, x, dy, y, dt, a2, seg, bm, cm, st_in, rin, skip):
    heads, tokens = dt.shape
    inner, state = x.shape[0], bm.shape[1]
    nb = tokens // QB
    lanes, per_head, sg, nat, full, sk, st = scan_specs(inner, heads, state, nb, True)
    return pl.pallas_call(
        functools.partial(scan_bwd_kernel, places, inner // len(places)),
        grid=(nb,),
        in_specs=[lanes, lanes, lanes, per_head, per_head, sg, nat, nat, st, full, sk],
        out_specs=[lanes, nat, nat, per_head, per_head],
        out_shape=[
            jax.ShapeDtypeStruct((inner, tokens), F32),
            jax.ShapeDtypeStruct((tokens, state), F32),
            jax.ShapeDtypeStruct((tokens, state), F32),
            jax.ShapeDtypeStruct((heads, tokens), F32),
            jax.ShapeDtypeStruct((heads, tokens), F32),
        ],
        scratch_shapes=[
            pltpu.VMEM((inner, state), F32),
            pltpu.VMEM((inner, QB), BF16),
            pltpu.VMEM((inner, QB), BF16),
            pltpu.VMEM((heads, QB), F32),
            pltpu.VMEM((heads, QB), F32),
            pltpu.VMEM((heads, QB), F32),
            pltpu.VMEM((heads, state), F32),
        ],
        compiler_params=params(),
        cost_estimate=pl.CostEstimate(
            flops=60 * inner * tokens * state, transcendentals=0, bytes_accessed=16 * x.size
        ),
    )(x, dy, y, dt, a2, seg, bm, cm, st_in, rin, skip)

def gather_kernel(
    ndp, nz, sc, hs, hw,
    x_ref, cot_ref, wv_in, wg_in, wo_in,
    states_ref, stepw_ref, cv_ref, cvb_ref, gg1_ref, heads_ref, cs_ref, csb_ref, gain_ref, len_ref,
    gv_ref, gs_ref, gg_ref, go_ref, pars_ref, nt_ref, ct_ref, vpre_ref, gpre_ref, vt_ref, st_ref, bc_ref,
    seg_ref, match_ref, ahead_ref, v_ref, dt_ref, a_ref, scale_ref, rates_ref, whole_ref, sin_ref,
    xbuf, nt, cbuf, ct, wv_ref, wg_ref, wo_ref, ws_ref, small_own, small_sib, par_ref, wvm, wsm, pvm, cols,
    scols, shifts, spre, st_low, vpre, gpre, vt,
    scaled, tails, fresh, hop_out, hop_in,
    z_send, full_recv, near_send, far_send, far_recv, misc_send, misc_recv, par_send, par_recv, local, load, out_sem,
    hop_send, hop_recv,
):
    nh, lo = 2 * nz, ndp // 2
    n, width = x_ref.shape
    tokens = 2 * n
    r, c = wv_in.shape
    dp, head = lax.axis_index("dp"), lax.axis_index("head")
    core, zed = lax.rem(head, 2), lax.div(head, 2)
    dhi, dlo = lax.div(dp, lo), lax.rem(dp, lo)
    sib = zed * 2 + 1 - core
    hi_peer = (1 - dhi) * lo + dlo
    lo_slots = [lax.rem(dlo + k, lo) for k in range(1, lo)]
    lo_peers = [dhi * lo + s for s in lo_slots]

    def half(rows, i):
        return pl.ds(0, rows // 32 * 16) if i == 0 else pl.ds(rows // 32 * 16, rows - rows // 32 * 16)

    order = [1] + [nz - 1] * (nz > 2) + list(range(2, nz - 1))

    barrier = pltpu.get_barrier_semaphore()
    partners = [(dp, lax.rem(head + k, nh)) for k in range(1, nh)]
    partners += [(p, head) for p in lo_peers + [hi_peer]]
    for partner in partners:
        pl.semaphore_signal(barrier, inc=1, device_id=partner, device_id_type=MESH)
    pl.semaphore_wait(barrier, len(partners))

    def remote(src, dst, send, recv, device):
        pltpu.make_async_remote_copy(
            src_ref=src, dst_ref=dst, send_sem=send, recv_sem=recv, device_id=device, device_id_type=MESH
        ).start()

    def wait_for(ref, sem):
        pltpu.make_async_copy(ref, ref, sem).wait()

    def along_z(m, own, slot):
        for k in range(1, nz):
            remote(
                own, slot, z_send.at[m, k], full_recv.at[m, dp, zed], (dp, lax.rem(zed + k, nz) * 2 + core)
            )

    def near(m, slots, zi, own=None):
        z = lax.rem(zed + zi, nz)
        if own is None:
            wait_for(slots.at[dp, z], full_recv.at[m, dp, z])
        src = slots.at[dp, z] if own is None else own
        for i, p in enumerate(lo_peers + [hi_peer]):
            remote(src, slots.at[dp, z], near_send.at[m, zi, i], full_recv.at[m, dp, z], (p, head))

    def far(m, slots, zi):
        z = lax.rem(zed + zi, nz)
        wait_for(slots.at[hi_peer, z], full_recv.at[m, hi_peer, z])
        for i, p in enumerate(lo_peers):
            part = slots.at[hi_peer, z, half(slots.shape[2], 0)]
            remote(part, part, far_send.at[m, zi, i], far_recv.at[m, hi_peer, z, 0], (p, head))
        for i, d in enumerate(lo_peers):
            wait_for(slots.at[d, z], full_recv.at[m, d, z])
            part = slots.at[d, z, half(slots.shape[2], 1)]
            remote(part, part, far_send.at[m, zi, lo - 1 + i], far_recv.at[m, d, z, 1], (hi_peer, head))

    def fetch(m, slots, vm, z):
        for s in lo_slots:
            d = (1 - dhi) * lo + s
            for i in range(2):
                wait_for(slots.at[d, z, half(slots.shape[2], i)], far_recv.at[m, d, z, i])
        for d in range(ndp):
            pltpu.make_async_copy(slots.at[d, z], vm.at[z, d], load.at[m, z, d]).start()

    def fetched(m, slots, vm, z):
        for d in range(ndp):
            pltpu.make_async_copy(slots.at[d, z], vm.at[z, d], load.at[m, z, d]).wait()

    def lanes(v, before):
        parts = [jnp.zeros((v.shape[0], before), F32)] * (before > 0) + [v.astype(F32)]
        return jnp.concatenate(parts + [jnp.zeros((v.shape[0], 128 - before - v.shape[1]), F32)], axis=1)

    wv_ref[...] = wv_in[...].T
    along_z(0, wv_ref, gv_ref.at[dp, zed])
    near(0, gv_ref, 0, wv_ref)
    small_t = pltpu.roll(lanes(states_ref[...], 0), core * sc, 1) + lanes(stepw_ref[...], 2 * sc)
    ws_ref[...] = small_t.T[0 : ws_ref.shape[0]].astype(BF16)
    remote(ws_ref, small_sib, misc_send.at[0], misc_recv.at[0], (dp, sib))
    own_rows = pl.ds(HALO + core * n, n)
    remote(x_ref, xbuf.at[own_rows], misc_send.at[1], misc_recv.at[1], (dp, sib))

    @pl.when((core == 1) & (zed < nz - 1))
    def _():
        for i in range(2):
            remote(
                x_ref.at[pl.ds(n - HALO, HALO)], xbuf.at[pl.ds(0, HALO)], misc_send.at[3 + i], misc_recv.at[3],
                (dp, (zed + 1) * 2 + i),
            )

    wg_ref[...] = wg_in[...].T
    wo_ref[...] = wo_in[...].T
    mine = [
        pltpu.make_async_copy(x_ref, xbuf.at[own_rows], local.at[0]),
        pltpu.make_async_copy(wv_ref, gv_ref.at[dp, zed], local.at[1]),
        pltpu.make_async_copy(wg_ref, gg_ref.at[dp, zed], local.at[2]),
        pltpu.make_async_copy(cot_ref, cbuf.at[pl.ds(core * n, n)], local.at[3]),
        pltpu.make_async_copy(wo_ref, go_ref.at[dp, zed], local.at[4]),
    ]
    for copy in mine:
        copy.start()

    wait_for(small_sib, misc_recv.at[0])
    line = lax.broadcasted_iota(jnp.int32, small_own.shape, 0)
    low_line = (1 - core) * sc
    theirs = (line >= low_line) & (line < low_line + sc)
    small_own[...] = jnp.where(
        theirs, small_sib[...].astype(F32), ws_ref[...].astype(F32)
    ).astype(BF16)
    along_z(1, small_own, gs_ref.at[dp, zed])
    near(1, gs_ref, 0, small_own)
    own_small = pltpu.make_async_copy(small_own, gs_ref.at[dp, zed], local.at[7])
    own_small.start()
    par_ref[...] = jnp.zeros(par_ref.shape, F32)
    par_ref[0:4] = cv_ref[...]
    par_ref[4:5] = cvb_ref[...]
    par_ref[5:6] = gg1_ref[...]
    par_ref[6:9, 0:128] = lanes(heads_ref[...], 0)
    par_ref[9:13, 0:128] = pltpu.roll(lanes(cs_ref[...], 0), core * sc, 1)
    par_ref[13:14, 0:128] = pltpu.roll(lanes(csb_ref[...], 0), core * sc, 1)
    own_par = pltpu.make_async_copy(par_ref, pars_ref.at[head], local.at[5])
    own_par.start()
    for k in range(1, nh):
        remote(par_ref, pars_ref.at[head], par_send.at[k], par_recv.at[head], (dp, lax.rem(head + k, nh)))
    remote(cot_ref, cbuf.at[pl.ds(core * n, n)], misc_send.at[2], misc_recv.at[2], (dp, sib))

    span = LH + tokens
    ends = [len_ref[0, 0]]
    for k in range(1, len_ref.shape[1]):
        ends.append(ends[-1] + len_ref[0, k])

    def segment(at):
        number = sum([(at >= end).astype(F32) for end in ends[1:]], (at >= ends[0]).astype(F32))
        return jnp.where((at < 0) | (at >= nz * tokens), -1.0, number)

    at = zed * tokens - LH + lax.broadcasted_iota(jnp.int32, (8, span), 1)
    tap = lax.broadcasted_iota(jnp.int32, (8, span), 0)
    number = segment(at)
    seg_ref[...] = number
    valid = (tap < 4) & (at >= zed * tokens)
    match_ref[...] = jnp.where(valid & (segment(at - 3 + tap) == number), 1.0, 0.0)
    ahead_ref[...] = jnp.where((tap < 4) & (segment(at + 3 - tap) == number), 1.0, 0.0)[:, LH:]

    def normalise(start, count):
        rows = xbuf[pl.ds(start, count), :].astype(F32)
        inverse = lax.rsqrt(jnp.mean(rows * rows, axis=1, keepdims=True) + EPSILON)
        return (rows * inverse * gain_ref[...]).astype(BF16)

    def normalise_half(which):
        @pl.loop(0, n // 128)
        def _(i):
            at = pl.multiple_of(which * n + i * 128, 128)
            nt[:, pl.ds(pl.multiple_of(LH + at, 128), 128)] = normalise(pl.multiple_of(HALO + at, 16), 128).T

    def turn(which):
        @pl.loop(0, n // 128)
        def _(i):
            at = pl.multiple_of(which * n + i * 128, 128)
            ct[:, pl.ds(at, 128)] = cbuf[pl.ds(at, 128), :].T

    mine[0].wait()
    normalise_half(core)
    near(0, gv_ref, order[0])
    wait_for(x_ref, misc_recv.at[1])
    normalise_half(1 - core)
    for zi in order[1:]:
        near(0, gv_ref, zi)
    along_z(2, wg_ref, gg_ref.at[dp, zed])
    for zi in order:
        near(1, gs_ref, zi)

    @pl.when(zed > 0)
    def _():
        wait_for(xbuf.at[pl.ds(0, HALO)], misc_recv.at[3])

    @pl.when(zed == 0)
    def _():
        xbuf[0:HALO, :] = jnp.zeros((HALO, width), BF16)

    before = normalise(0, HALO).astype(F32)
    nt[:, 0:LH] = jnp.concatenate([jnp.zeros((LH - HALO, width), F32), before], axis=0).astype(BF16).T
    out_nt = pltpu.make_async_copy(nt.at[:, pl.ds(LH, tokens)], nt_ref, out_sem.at[3 * nz])
    out_nt.start()
    far(0, gv_ref, 0)
    far(1, gs_ref, 0)
    mine[3].wait()
    turn(core)
    for zi in order:
        far(0, gv_ref, zi)
        far(1, gs_ref, zi)
    near(2, gg_ref, 0, wg_ref)

    for k in range(1, nh):
        other = lax.rem(head + k, nh)
        wait_for(pars_ref.at[other], par_recv.at[other])
    own_par.wait()
    get_pars = pltpu.make_async_copy(pars_ref, pvm, local.at[5])
    get_pars.start()
    wait_for(cot_ref, misc_recv.at[2])
    turn(1 - core)
    get_pars.wait()
    out_ct = pltpu.make_async_copy(ct, ct_ref, out_sem.at[3 * nz + 1])
    out_ct.start()

    own_small.wait()
    mine[1].wait()
    for z in range(nz):
        fetch(1, gs_ref, wsm, z)
    for z in range(nz):
        fetch(0, gv_ref, wvm, z)
    place = lax.broadcasted_iota(jnp.int32, (256, 128), 0) - lax.broadcasted_iota(jnp.int32, (256, 128), 1)

    @pl.loop(0, tokens // 128)
    def _(b):
        at = pl.ds(pl.multiple_of(LH + b * 128, 128), 128)
        for k in range(3):
            shifts[b, :, k * 128 : k * 128 + 128] = jnp.where(
                place == 125 + k, match_ref[k : k + 1, at], 0.0
            ).astype(BF16)

    lanes_chunk = chunk_of(span, 384, 128)

    def by_width(weights, z):
        return jnp.concatenate([weights[z, d] for d in range(ndp)], axis=1)

    def shift(source, count, rest=None):
        @pl.loop(0, tokens // 128)
        def _(b):
            wide = pl.ds(pl.multiple_of(b * 128, 128), 256)
            moved = mm(source[:, wide], shifts[b], 1, 0)
            if rest is not None:
                moved = moved + mm(rest[:, wide], shifts[b], 1, 0)
            for k in range(3):
                gpre[k, 0:count, pl.ds(pl.multiple_of(b * 128, 128), 128)] = moved[:, k * 128 : k * 128 + 128]

    def convolved(source, taps, rows, base, rest=None):
        at = pl.ds(base, 256)
        here = source[rows, pl.ds(LH + base, 256)].astype(F32)
        if rest is not None:
            here = here + rest[rows, pl.ds(LH + base, 256)].astype(F32)
        pre = taps[:, 3:4] * here + taps[:, 4:5]
        for k in range(3):
            pre = pre + taps[:, k : k + 1] * gpre[k, rows, at]
        return pre * sigmoid(pre)

    for z in range(nz):
        fetched(1, gs_ref, wsm, z)

    @pl.loop(0, span // lanes_chunk)
    def _(i):
        at = pl.ds(pl.multiple_of(i * lanes_chunk, 128), lanes_chunk)
        left = jnp.concatenate([by_width(wsm, z) for z in range(nz)], axis=0)
        spre[:, at] = mm(left, nt[:, at], 1, 0)

    sr = wsm.shape[2]
    for z in range(nz):
        part = slice(z * 2 * sc, (z + 1) * 2 * sc)
        here = spre[z * sr : z * sr + 2 * sc, :]
        high = here.astype(BF16)
        st_ref[part, :] = high
        st_low[part, :] = (here - high.astype(F32)).astype(BF16)
        v_ref[z * 8 : z * 8 + 8, :] = spre[z * sr + 2 * sc : z * sr + 2 * sc + 8, LH:]
        both = pvm[2 * z, 8:16, 0:128] + pvm[2 * z + 1, 8:16, 0:128]
        scols[part, :] = both.T[0 : 2 * sc, 1:6]
    bc_rows = 2 * sc * nz
    shift(st_ref, bc_rows, st_low)

    @pl.loop(0, bc_rows // 32, unroll=2)
    def _(g):
        rows = pl.ds(pl.multiple_of(g * 32, 32), 32)
        taps = scols[rows, :]
        for base in range(0, tokens, 256):
            scaled[rows, pl.ds(base, 256)] = convolved(st_ref, taps, rows, base, st_low).astype(BF16)

    @pl.loop(0, tokens // 128)
    def _(b):
        at = pl.ds(pl.multiple_of(b * 128, 128), 128)
        for i in range(2):
            bc_ref[i, at, :] = scaled[i * 128 : i * 128 + 128, at].T

    columns = [pvm[2 * z + core, 0:16, 0:128].T[0:8] for z in range(nz)]

    def column(k):
        return jnp.concatenate([v[:, k : k + 1] for v in columns], axis=0)

    v = v_ref[...] + column(6)
    v_ref[...] = v
    dt = jnp.maximum(v, 0.0) + jnp.log1p(jnp.exp(-jnp.abs(v)))
    dt_ref[...] = dt
    rates = -jnp.exp(column(7))
    rates_ref[...] = jnp.broadcast_to(rates, rates_ref.shape)
    a2 = dt * (rates * LOG2E)
    a_ref[...] = a2
    segr = seg_ref[0:1, LH:]
    last, first = segr[:, tokens - 1 :], seg_ref[0:1, LH - 1 : LH]
    before = lane_cumsum(a2)
    through = before[:, tokens - 1 :]
    scale_ref[...] = jnp.where(segr == first, jnp.exp2(before), 0.0)
    whole_ref[...] = jnp.broadcast_to(jnp.where(last == first, jnp.exp2(through), 0.0), whole_ref.shape)
    tail = jnp.where(segr == last, jnp.exp2(lane_cumsum(a2, True) - a2) * dt, 0.0)
    tails[...] = tail

    for z in range(nz):
        fetched(0, gv_ref, wvm, z)

    @pl.loop(0, nz)
    def _(z):
        cols[...] = pvm[2 * z + core, 0:8, :].T

        @pl.loop(0, span // lanes_chunk)
        def _(i):
            at = pl.ds(pl.multiple_of(i * lanes_chunk, 128), lanes_chunk)
            vpre[z, :, at] = mm(by_width(wvm, z), nt[:, at], 1, 0).astype(BF16)

        pltpu.make_async_copy(vpre.at[z], vpre_ref.at[z], out_sem.at[z]).start()
        shift(vpre.at[z], c)

        @pl.loop(0, c // 32, unroll=2)
        def _(g):
            rows = pl.ds(pl.multiple_of(g * 32, 32), 32)
            taps = cols[rows, :]
            decay = pl.ds(z * 8 + g // (hw // 32), 1)
            for base in range(0, tokens, 256):
                at = pl.ds(base, 256)
                low = convolved(vpre.at[z], taps, rows, base).astype(BF16)
                vt[z, rows, at] = low
                scaled[rows, at] = (low.astype(F32) * tails[decay, at]).astype(BF16)

        pltpu.make_async_copy(vt.at[z], vt_ref.at[z], out_sem.at[nz + z]).start()
        fresh[z] = mm(scaled[0:c, :], bc_ref[0], 1, 0)

        @pl.when(z < nz - 1)
        def _():
            near(2, gg_ref, z + 1)

        @pl.when(z > 0)
        def _():
            far(2, gg_ref, z - 1)

        @pl.when(z == 1)
        def _():
            along_z(3, wo_ref, go_ref.at[dp, zed])

    far(2, gg_ref, nz - 1)

    mine[2].wait()
    near(3, go_ref, 0, wo_ref)
    for z in range(nz):
        fetch(2, gg_ref, wvm, z)
    gate_chunk = chunk_of(tokens, 512, 128)

    def hop(i):
        if i:
            hop_arrived(i - 1)
            for z in range(nz):
                for h in range(hs):
                    at = slice(h * hw, (h + 1) * hw)
                    state = whole_ref[z * 8 + h : z * 8 + h + 1, :] * hop_in[i - 1, z, at, :].astype(F32)
                    hop_out[i, z, at, :] = (fresh[z, at, :] + state).astype(BF16)
        else:
            hop_out[0] = fresh[...].astype(BF16)

        @pl.when(zed < nz - 1)
        def _():
            remote(hop_out.at[i], hop_in.at[i], hop_send.at[i], hop_recv.at[i], (dp, (zed + 1) * 2 + core))

    def hop_arrived(i):
        @pl.when(zed > 0)
        def _():
            wait_for(hop_in.at[i], hop_recv.at[i])

        @pl.when(zed == 0)
        def _():
            hop_in[i] = jnp.zeros(hop_in.shape[1:], BF16)

    hops = nz // 2
    for i in range(hops):
        hop(i)
        if i == 0:
            for zi in order:
                near(3, go_ref, zi)
        for z in (2 * i, 2 * i + 1):
            fetched(2, gg_ref, wvm, z)

        @pl.loop(2 * i, 2 * i + 2)
        def _(z):
            @pl.loop(0, tokens // gate_chunk)
            def _(i):
                at = pl.multiple_of(i * gate_chunk, 128)
                right = nt[:, pl.ds(pl.multiple_of(LH + at, 128), gate_chunk)]
                gpre[z, 0:c, pl.ds(at, gate_chunk)] = mm(by_width(wvm, z), right, 1, 0)

            pltpu.make_async_copy(gpre.at[z, pl.ds(0, c)], gpre_ref.at[z], out_sem.at[2 * nz + z]).start()

    for zi in [0] + order:
        far(3, go_ref, zi)
    hop_arrived(hops - 1)
    sin_ref[...] = hop_in[hops - 1]

    @pl.when(zed < nz - 1)
    def _():
        for i in range(hops):
            wait_for(hop_out.at[i], hop_send.at[i])

    mine[4].wait()
    for z in range(nz):
        for s in lo_slots:
            d = (1 - dhi) * lo + s
            for i in range(2):
                wait_for(go_ref.at[d, z, half(c, i)], far_recv.at[3, d, z, i])
    sent = [wv_ref, small_own, wg_ref, wo_ref]
    for m in range(4):
        for k in range(1, nz):
            wait_for(sent[m], z_send.at[m, k])
    for m in range(4):
        for zi in range(nz):
            for i in range(lo):
                wait_for(sent[m], near_send.at[m, zi, i])
            for i in range(2 * (lo - 1)):
                wait_for(sent[m].at[half(sent[m].shape[0], i // (lo - 1))], far_send.at[m, zi, i])
    wait_for(ws_ref, misc_send.at[0])
    wait_for(x_ref, misc_send.at[1])
    wait_for(cot_ref, misc_send.at[2])
    for k in range(1, nh):
        wait_for(par_ref, par_send.at[k])

    @pl.when((core == 1) & (zed < nz - 1))
    def _():
        for i in range(2):
            wait_for(x_ref.at[pl.ds(n - HALO, HALO)], misc_send.at[3 + i])

    for z in range(nz):
        pltpu.make_async_copy(vpre.at[z], vpre_ref.at[z], out_sem.at[z]).wait()
        pltpu.make_async_copy(vt.at[z], vt_ref.at[z], out_sem.at[nz + z]).wait()
        pltpu.make_async_copy(gpre.at[z, pl.ds(0, c)], gpre_ref.at[z], out_sem.at[2 * nz + z]).wait()
    out_nt.wait()
    out_ct.wait()


def gather_project(
    ndp, nz, sc, hs, hw, x, cot, wv, wg, wo, states, stepw, cv, cvb, gg, heads, cs, csb, gain, lengths
):
    n, width = x.shape
    tokens = 2 * n
    r, c = wv.shape
    nh, lo, hops = 2 * nz, ndp // 2, nz // 2
    sr, most = 2 * sc + 16, max(c, 2 * sc * nz)
    anywhere = pl.BlockSpec(memory_space=pl.ANY)
    vmem = pl.BlockSpec(memory_space=pltpu.VMEM)
    dma = pltpu.SemaphoreType.DMA
    return pl.pallas_call(
        functools.partial(gather_kernel, ndp, nz, sc, hs, hw),
        in_specs=[anywhere] * 2 + [vmem] * 12 + [pl.BlockSpec(memory_space=pltpu.SMEM)],
        out_specs=[anywhere] * 10 + [vmem] * 12,
        out_shape=[
            shape((ndp, nz, c, r), BF16),
            shape((ndp, nz, sr, r), BF16),
            shape((ndp, nz, c, r), BF16),
            shape((ndp, nz, c, r), BF16),
            shape((nh, 16, c), F32),
            shape((width, tokens), BF16),
            shape((width, tokens), BF16),
            shape((nz, c, LH + tokens), BF16),
            shape((nz, c, tokens), F32),
            shape((nz, c, tokens), BF16),
            shape((2 * sc * nz, LH + tokens), BF16),
            shape((2, tokens, 128), BF16),
            shape((8, LH + tokens), F32),
            shape((8, LH + tokens), F32),
            shape((8, tokens), F32),
            shape((nz * 8, tokens), F32),
            shape((nz * 8, tokens), F32),
            shape((nz * 8, tokens), F32),
            shape((nz * 8, tokens), F32),
            shape((nz * 8, 128), F32),
            shape((nz * 8, 128), F32),
            shape((nz, c, 128), BF16),
        ],
        scratch_shapes=[
            pltpu.VMEM((HALO + tokens, width), BF16),
            pltpu.VMEM((width, LH + tokens), BF16),
            pltpu.VMEM((tokens, width), BF16),
            pltpu.VMEM((width, tokens), BF16),
            pltpu.VMEM((c, r), BF16),
            pltpu.VMEM((c, r), BF16),
            pltpu.VMEM((c, r), BF16),
            pltpu.VMEM((sr, r), BF16),
            pltpu.VMEM((sr, r), BF16),
            pltpu.VMEM((sr, r), BF16),
            pltpu.VMEM((16, c), F32),
            pltpu.VMEM((nz, ndp, c, r), BF16),
            pltpu.VMEM((nz, ndp, sr, r), BF16),
            pltpu.VMEM((nh, 16, c), F32),
            pltpu.VMEM((c, 8), F32),
            pltpu.VMEM((2 * sc * nz, 5), F32),
            pltpu.VMEM((tokens // 128, 256, 384), BF16),
            pltpu.VMEM((nz * sr, LH + tokens), F32),
            pltpu.VMEM((2 * sc * nz, LH + tokens), BF16),
            pltpu.VMEM((nz, c, LH + tokens), BF16),
            pltpu.VMEM((nz, most, tokens), F32),
            pltpu.VMEM((nz, c, tokens), BF16),
            pltpu.VMEM((most, tokens), BF16),
            pltpu.VMEM((nz * 8, tokens), F32),
            pltpu.VMEM((nz, c, 128), F32),
            pltpu.VMEM((hops, nz, c, 128), BF16),
            pltpu.VMEM((hops, nz, c, 128), BF16),
            dma((4, nz)),
            dma((4, ndp, nz)),
            dma((4, nz, lo)),
            dma((4, nz, 2 * (lo - 1))),
            dma((4, ndp, nz, 2)),
            dma((5,)),
            dma((4,)),
            dma((nh,)),
            dma((nh,)),
            dma((8,)),
            dma((3, nz, ndp)),
            dma((3 * nz + 2,)),
            dma((hops,)),
            dma((hops,)),
        ],
        compiler_params=pltpu.CompilerParams(
            collective_id=1, has_side_effects=True, vmem_limit_bytes=60 * MIB
        ),
        cost_estimate=cost(2 * tokens * width * nz * (2 * c + 128), 60 * MIB),
    )(x, cot, wv, wg, wo, states, stepw, cv, cvb, gg, heads, cs, csb, gain, lengths)

def mix_kernel(ndp, wo_ref, ct_ref, y_ref, g_ref, gain_ref, gated_ref, h1_ref, sums_ref, acc, low):
    c, tokens = y_ref.shape
    z = pl.program_id(0)
    chunk = chunk_of(tokens, 512, 128)

    @pl.loop(0, tokens // chunk)
    def _(i):
        at = pl.ds(pl.multiple_of(i * chunk, 128), chunk)
        left = jnp.concatenate([wo_ref[d, 0] for d in range(ndp)], axis=1)
        h1_ref[:, at] = mm(left, ct_ref[:, at], 1, 0)

    @pl.when(z == 0)
    def _():
        acc[...] = jnp.zeros(acc.shape, F32)

    @pl.loop(0, c // 16, unroll=2)
    def _(i):
        rows = pl.ds(pl.multiple_of(i * 16, 16), 16)
        scale = gain_ref[rows, :]
        for at in lane_chunks(tokens):
            g = g_ref[rows, at]
            mixed = y_ref[rows, at] * (g * sigmoid(g))
            gated = (mixed * scale).astype(BF16)
            low[rows, at] = gated
            square = mixed * mixed
            dots = gated.astype(F32) * h1_ref[rows, at]
            acc[0:8, at] += square[0:8] + square[8:16]
            acc[8:16, at] += dots[0:8] + dots[8:16]

    gated_ref[0] = low[...].T

    @pl.when(z == pl.num_programs(0) - 1)
    def _():
        sums_ref[0:1] = jnp.sum(acc[0:8], axis=0, keepdims=True)
        sums_ref[1:2] = jnp.sum(acc[8:16], axis=0, keepdims=True)
        sums_ref[2:8] = jnp.zeros((6, tokens), F32)


def mix(wo, ct, y, g, gain):
    ndp, nz, c, r = wo.shape
    width, tokens = ct.shape
    inner = nz * c
    block = pl.BlockSpec((c, tokens), lambda z: (z, 0))
    return pl.pallas_call(
        functools.partial(mix_kernel, ndp),
        grid=(nz,),
        in_specs=[
            pl.BlockSpec((ndp, 1, c, r), lambda z: (0, z, 0, 0)),
            pl.BlockSpec((width, tokens), lambda z: (0, 0)),
            block, block,
            pl.BlockSpec((c, 1), lambda z: (z, 0)),
        ],
        out_specs=[
            pl.BlockSpec((1, tokens, c), lambda z: (z, 0, 0)), block, pl.BlockSpec((8, tokens), lambda z: (0, 0)),
        ],
        out_shape=[shape((nz, tokens, c), BF16), shape((inner, tokens), F32), shape((8, tokens), F32)],
        scratch_shapes=[pltpu.VMEM((16, tokens), F32), pltpu.VMEM((c, tokens), BF16)],
        compiler_params=params(),
        cost_estimate=cost(2 * inner * tokens * width, 22 * inner * tokens),
    )(wo, ct, y, g, gain)


def unmix_kernel(
    ndp, nz, hs, hw, total,
    y_ref, g_ref, h1_ref, x_ref, gain_ref, sums_ref, scale_ref, cm_ref, whole_ref, nt_ref,
    dy_ref, gl_ref, cols_ref, grad_ref, rin_ref,
    scaled, acc, low, turned, back, hop_out, hop_in, hop_send, hop_recv,
):
    c = y_ref.shape[0]
    hops = nz // 2
    step = pl.program_id(0)
    dp, head = lax.axis_index("dp"), lax.axis_index("head")
    core, zed = lax.rem(head, 2), lax.div(head, 2)

    @pl.when(step == 0)
    def _():
        barrier = pltpu.get_barrier_semaphore()
        for k in range(1, nz):
            pl.semaphore_signal(
                barrier, inc=1, device_id=(dp, lax.rem(zed + k, nz) * 2 + core), device_id_type=MESH
            )
        pl.semaphore_wait(barrier, nz - 1)

    @pl.when(step < nz)
    def _():
        inverse = lax.rsqrt(sums_ref[0:1] / total + EPSILON)
        weight = sums_ref[1:2] * (inverse * inverse * inverse) / total

        @pl.loop(0, c // 16, unroll=2)
        def _(i):
            rows = pl.ds(pl.multiple_of(i * 16, 16), 16)
            gain = gain_ref[rows, :]
            head_row = pl.ds(i // (hw // 16), 1)
            gains, skips = [], []
            for at in lane_chunks(y_ref.shape[1]):
                y, g = y_ref[rows, at], g_ref[rows, at]
                sig = sigmoid(g)
                silu = g * sig
                mixed = y * silu
                gated_grad = h1_ref[rows, at] * inverse[:, at]
                mixed_grad = gated_grad * gain - weight[:, at] * mixed
                dy = (mixed_grad * silu).astype(BF16)
                dy_ref[rows, at] = dy
                low[rows, at] = (mixed_grad * y * (sig + silu * (1.0 - sig))).astype(BF16)
                dyf = dy.astype(F32)
                scaled[rows, at] = (dyf * scale_ref[head_row, at]).astype(BF16)
                gains.append(folded(gated_grad * mixed))
                skips.append(folded(dyf * x_ref[rows, at].astype(F32)))
            acc[0, rows, :] = sum(gains[1:], gains[0])
            acc[1, rows, :] = sum(skips[1:], skips[0])

        for k in range(2):
            cols_ref[0, k : k + 1] = jnp.sum(acc[k].T, axis=0, keepdims=True)
        cols_ref[0, 2:8] = jnp.zeros((6, c), F32)
        flipped = low[...].T
        gl_ref[0] = flipped
        turned[step] = flipped
        back[step] = mm(scaled[...], cm_ref[...], 1, 0)

    def hop_arrived(i, z):
        @pl.when(zed < nz - 1)
        def _():
            pltpu.make_async_copy(hop_in.at[i, z], hop_in.at[i, z], hop_recv.at[i, z]).wait()

        @pl.when(zed == nz - 1)
        def _():
            hop_in[i, z] = jnp.zeros(hop_in.shape[2:], BF16)

    def hop(i, z):
        if i:
            hop_arrived(i - 1, z)
            for h in range(hs):
                at = slice(h * hw, (h + 1) * hw)
                state = whole_ref[pl.ds(z * 8 + h, 1), :] * hop_in[i - 1, z, at, :].astype(F32)
                hop_out[i, z, at, :] = (back[z, at, :] + state).astype(BF16)
        else:
            hop_out[0, z] = back[z].astype(BF16)

        @pl.when(zed > 0)
        def _():
            pltpu.make_async_remote_copy(
                src_ref=hop_out.at[i, z], dst_ref=hop_in.at[i, z],
                send_sem=hop_send.at[i, z], recv_sem=hop_recv.at[i, z],
                device_id=(dp, (zed - 1) * 2 + core), device_id_type=MESH,
            ).start()

    @pl.when(step >= nz)
    def _():
        r = nt_ref.shape[0] // ndp
        right = turned[step - nz]
        for d in range(ndp):
            grad_ref[d, 0] = mm(nt_ref[d * r : (d + 1) * r, :], right, 1, 0).astype(BF16)

    for i in range(hops):
        @pl.when((step >= 2 * i) & (step < nz + 2 * i))
        def _(i=i):
            hop(i, step - 2 * i)

    @pl.when(step == 2 * nz - 1)
    def _():
        for z in range(nz):
            hop_arrived(hops - 1, z)
        rin_ref[...] = hop_in[hops - 1]

        @pl.when(zed > 0)
        def _():
            for i in range(hops):
                for z in range(nz):
                    pltpu.make_async_copy(hop_out.at[i, z], hop_out.at[i, z], hop_send.at[i, z]).wait()


def unmix(ndp, nz, hs, hw, y, g, h1, x, gain, sums, scale, cm, whole, nt):
    inner, tokens = y.shape
    c = inner // nz
    state = cm.shape[1]
    width = nt.shape[0]
    hops = nz // 2

    def first(s):
        return jnp.minimum(s, nz - 1)

    def second(s):
        return jnp.maximum(s - nz, 0)

    block = pl.BlockSpec((c, tokens), lambda s: (first(s), 0))
    dma = pltpu.SemaphoreType.DMA

    def fixed(v):
        return pl.BlockSpec(v.shape, lambda s: (0,) * v.ndim)

    return pl.pallas_call(
        functools.partial(unmix_kernel, ndp, nz, hs, hw, inner * 2),
        grid=(2 * nz,),
        in_specs=[
            block, block, block, block,
            pl.BlockSpec((c, 1), lambda s: (first(s), 0)),
            fixed(sums),
            pl.BlockSpec((8, tokens), lambda s: (first(s), 0)),
            fixed(cm), fixed(whole), fixed(nt),
        ],
        out_specs=[
            block,
            pl.BlockSpec((1, tokens, c), lambda s: (first(s), 0, 0)),
            pl.BlockSpec((1, 8, c), lambda s: (first(s), 0, 0)),
            pl.BlockSpec((ndp, 1, width // ndp, c), lambda s: (0, second(s), 0, 0)),
            pl.BlockSpec((nz, c, state), lambda s: (0, 0, 0)),
        ],
        out_shape=[
            shape((inner, tokens), BF16), shape((nz, tokens, c), BF16), shape((nz, 8, c), F32),
            shape((ndp, nz, width // ndp, c), BF16), shape((nz, c, state), BF16),
        ],
        scratch_shapes=[
            pltpu.VMEM((c, tokens), BF16), pltpu.VMEM((2, c, 128), F32), pltpu.VMEM((c, tokens), BF16),
            pltpu.VMEM((nz, tokens, c), BF16), pltpu.VMEM((nz, c, state), F32),
            pltpu.VMEM((hops, nz, c, state), BF16), pltpu.VMEM((hops, nz, c, state), BF16),
            dma((hops, nz)), dma((hops, nz)),
        ],
        compiler_params=pltpu.CompilerParams(
            collective_id=4, has_side_effects=True, vmem_limit_bytes=56 * MIB
        ),
        cost_estimate=cost(2 * inner * tokens * (state + width), 28 * inner * tokens),
    )(y, g, h1, x, gain, sums, scale, cm, whole, nt)


def weight_grad_kernel(ndp, total, *refs):
    left_ref, right_ref = refs[0], refs[1]
    r = left_ref.shape[0] // ndp
    if total:
        sums_ref, out_ref, left = refs[2:]

        @pl.when(pl.program_id(0) == 0)
        def _():
            inverse = lax.rsqrt(sums_ref[0:1] / total + EPSILON)

            @pl.loop(0, left.shape[0] // 64)
            def _(i):
                rows = pl.ds(pl.multiple_of(i * 64, 64), 64)
                left[rows, :] = (left_ref[rows, :].astype(F32) * inverse).astype(BF16)
    else:
        out_ref, left = refs[2], left_ref
    for d in range(ndp):
        out_ref[d, 0] = mm(left[d * r : (d + 1) * r, :], right_ref[0], 1, 0).astype(BF16)


def weight_grad(ndp, left, right, sums=None):
    width, tokens = left.shape
    nz, _, c = right.shape
    r, inner = width // ndp, nz * c
    operands = [left, right]
    specs = [pl.BlockSpec((width, tokens), lambda z: (0, 0)), pl.BlockSpec((1, tokens, c), lambda z: (z, 0, 0))]
    scratch = []
    if sums is not None:
        operands.append(sums)
        specs.append(pl.BlockSpec((8, tokens), lambda z: (0, 0)))
        scratch = [pltpu.VMEM((width, tokens), BF16)]
    return pl.pallas_call(
        functools.partial(weight_grad_kernel, ndp, 0 if sums is None else inner * 2),
        grid=(nz,),
        in_specs=specs,
        out_specs=pl.BlockSpec((ndp, 1, r, c), lambda z: (0, z, 0, 0)),
        out_shape=shape((ndp, nz, r, c), BF16),
        scratch_shapes=scratch,
        compiler_params=params(),
        cost_estimate=cost(2 * inner * tokens * width, 8 * inner * tokens),
    )(*operands)


def back_project_kernel(nz, n, weight_ref, right_ref, keep_ref, send_ref):
    core = lax.rem(lax.axis_index("head"), 2)
    weight = jnp.concatenate([weight_ref[0, z] for z in range(nz)], axis=0)

    def product(which):
        at = pl.ds(pl.multiple_of(which * n, 128), n)
        return mm(jnp.concatenate([right_ref[z, at, :] for z in range(nz)], axis=1), weight, 1, 0)

    send_ref[0] = product(1 - core).astype(BF16)
    keep_ref[0] = product(core)


def back_project(weight, right):
    ndp, nz, c, r = weight.shape
    tokens = right.shape[1]
    n = tokens // 2
    return pl.pallas_call(
        functools.partial(back_project_kernel, nz, n),
        grid=(ndp,),
        in_specs=[
            pl.BlockSpec((1, nz, c, r), lambda d: (d, 0, 0, 0)),
            pl.BlockSpec(right.shape, lambda d: (0, 0, 0)),
        ],
        out_specs=[pl.BlockSpec((1, n, r), lambda d: (d, 0, 0))] * 2,
        out_shape=[shape((ndp, n, r), F32), shape((ndp, n, r), BF16)],
        compiler_params=params(),
        cost_estimate=cost(2 * weight.size * tokens, 2 * right.size),
    )(weight, right)


def result_kernel(total, keep_ref, got_ref, sums_ref, x_ref, out_ref):
    inverse = lax.rsqrt(sums_ref[...].T[:, 0:1] / total + EPSILON)
    blocks = [keep_ref[d] + got_ref[d].astype(F32) for d in range(keep_ref.shape[0])]
    branch = jnp.concatenate(blocks, axis=1)
    out_ref[...] = (x_ref[...].astype(F32) + branch * inverse).astype(BF16)


def result(total, keep, got, sums, x):
    n, width = x.shape
    ndp, _, r = keep.shape
    blocks = pl.BlockSpec((ndp, 128, r), lambda i: (0, i, 0))
    rows = pl.BlockSpec((128, width), lambda i: (i, 0))
    return pl.pallas_call(
        functools.partial(result_kernel, total),
        grid=(n // 128,),
        in_specs=[blocks, blocks, pl.BlockSpec((8, 128), lambda i: (0, i)), rows],
        out_specs=rows,
        out_shape=shape((n, width), BF16),
        compiler_params=params(),
        cost_estimate=cost(0, 12 * n * width),
    )(keep, got, sums, x)


def conv_back_kernel(
    nz, sc,
    dx_hbm, p_hbm, db_hbm, dc_hbm, st_hbm,
    pars, match, ahead, v_ref, dt_ref, xdx_ref, da_ref, rates_ref, mix_ref,
    vl, small_t, table_ref,
    st, dstates, e, p, cols, scols, shifts, moved, acc, queue, squeue, heads, halo, sheads, shalo, turn, slanes,
    load, e_load, ds_send, ds_recv, halo_send, halo_recv,
):
    nh = 2 * nz
    _, c, wide = queue.shape
    tokens = wide - 128
    sr = 2 * sc + 16
    dp, head = lax.axis_index("dp"), lax.axis_index("head")
    core, zed = lax.rem(head, 2), lax.div(head, 2)

    def column_loads(z):
        at = pl.ds(pl.multiple_of(z * c, 16), c)
        return [
            pltpu.make_async_copy(dx_hbm.at[at], e.at[pl.ds(0, c)], e_load.at[0]),
            pltpu.make_async_copy(p_hbm.at[at], p, e_load.at[1]),
        ]

    for copy in column_loads(0):
        copy.start()
    loads = [
        pltpu.make_async_copy(a, b, load.at[i])
        for i, (a, b) in enumerate([(st_hbm, st), (db_hbm, dstates.at[0]), (dc_hbm, dstates.at[1])])
    ]
    for copy in loads:
        copy.start()

    barrier = pltpu.get_barrier_semaphore()
    for k in range(1, nh):
        pl.semaphore_signal(barrier, inc=1, device_id=(dp, lax.rem(head + k, nh)), device_id_type=MESH)
    pl.semaphore_wait(barrier, nh - 1)

    def remote(src, dst, send_sem, recv_sem, device):
        pltpu.make_async_remote_copy(
            src_ref=src, dst_ref=dst, send_sem=send_sem, recv_sem=recv_sem, device_id=device, device_id_type=MESH
        ).start()

    def wait_for(ref, sem):
        pltpu.make_async_copy(ref, ref, sem).wait()

    for i, ref in enumerate((db_hbm, dc_hbm)):
        remote(ref, dstates.at[2 + i], ds_send.at[i], ds_recv.at[i], (dp, zed * 2 + 1 - core))

    place = lax.broadcasted_iota(jnp.int32, (256, 128), 0) - lax.broadcasted_iota(jnp.int32, (256, 128), 1)

    def build_shifts(mask, first, before):
        @pl.loop(0, tokens // 128)
        def _(b):
            at = pl.ds(pl.multiple_of(before + b * 128, 128), 128)
            for k in range(3):
                shifts[b, :, k * 128 : k * 128 + 128] = jnp.where(
                    place == first(k), mask[k : k + 1, at], 0.0
                ).astype(BF16)

    def shift(source, count):
        @pl.loop(0, tokens // 128)
        def _(b):
            at = pl.multiple_of(b * 128, 128)
            out = mm(source[:, pl.ds(at, 256)], shifts[b], 1, 0).astype(BF16)
            for k in range(3):
                moved[k, 0:count, pl.ds(at, 128)] = out[:, k * 128 : k * 128 + 128]

    def slopes(source, taps, rows, base, grad):
        at = pl.ds(base, 256)
        terms = [moved[k, rows, at].astype(F32) for k in range(3)]
        terms.append(source[rows, pl.ds(LH + base, 256)].astype(F32))
        pre = taps[:, 4:5]
        for k in range(4):
            pre = pre + taps[:, k : k + 1] * terms[k]
        sig = sigmoid(pre)
        q = grad * (sig * (1.0 + pre * (1.0 - sig)))
        return q, [folded(q * term) for term in terms] + [folded(q)]

    def line_sums(count, to):
        for k in range(5):
            to(k)[...] = jnp.sum(acc[k, 0:count].T, axis=0, keepdims=True)

    build_shifts(match, lambda k: 125 + k, LH)

    @pl.loop(0, nz)
    def _(z):
        for copy in column_loads(z):
            copy.wait()
        cols[...] = pars[2 * z + core, 0:8, :].T
        shift(p, c)

        @pl.loop(0, c // 16, unroll=2)
        def _(i):
            rows_at = pl.ds(pl.multiple_of(i * 16, 16), 16)
            taps = cols[rows_at, :]
            totals = None
            for base in range(0, tokens, 256):
                q, terms = slopes(p, taps, rows_at, base, e[rows_at, pl.ds(base, 256)])
                queue[z, rows_at, pl.ds(base, 256)] = q.astype(BF16)
                totals = terms if totals is None else [a + b for a, b in zip(totals, terms)]
            for k in range(5):
                acc[k, rows_at, :] = totals[k]

        @pl.when(z < nz - 1)
        def _():
            for copy in column_loads(z + 1):
                copy.start()

        heads[z] = queue[z, :, 0:128].astype(F32).T[0:8]

        @pl.when(zed > 0)
        def _():
            remote(
                heads.at[z], halo.at[z], halo_send.at[z], halo_recv.at[z], (dp, (zed - 1) * 2 + core)
            )

        line_sums(c, lambda k: table_ref.at[z, k : k + 1])
        table_ref[z, 5:6] = mix_ref[z, 0:1]
        table_ref[z, 6:16] = jnp.zeros((10, c), F32)
        table_ref[z, 8:9] = mix_ref[z, 1:2]

    count = nz * 8
    da, dt, rates = da_ref[...], dt_ref[...], rates_ref[:, 0:1]
    step_grad = jnp.where(dt > TINY, xdx_ref[...] / jnp.maximum(dt, TINY), 0.0) + rates * da
    steps_grad = step_grad * sigmoid(v_ref[...])
    for k, v in ((6, steps_grad), (7, rates * (dt * da))):
        padded = folded(v)
        if count < 128:
            padded = jnp.concatenate([padded, jnp.zeros((128 - count, 128), F32)], axis=0)
        line = jnp.sum(padded.T, axis=0, keepdims=True)
        for z in range(nz):
            table_ref[z, k : k + 1, 0:128] = line[:, 0:128]
    steps_low = steps_grad.astype(BF16)

    for i in range(3):
        loads[i].wait()
    for i in range(2):
        wait_for(dstates.at[2 + i], ds_recv.at[i])
    for z in range(nz):
        both = pars[2 * z, 8:16, 0:128] + pars[2 * z + 1, 8:16, 0:128]
        scols[z * 2 * sc : (z + 1) * 2 * sc, :] = both.T[0 : 2 * sc, 1:6]

    @pl.loop(0, tokens // 128)
    def _(b):
        at = pl.ds(pl.multiple_of(b * 128, 128), 128)
        for i in range(2):
            e[i * 128 : i * 128 + 128, at] = (dstates[i, at, :] + dstates[2 + i, at, :]).T

    bc_rows = 2 * sc * nz
    shift(st, bc_rows)

    @pl.loop(0, bc_rows // 16, unroll=2)
    def _(i):
        rows_at = pl.ds(pl.multiple_of(i * 16, 16), 16)
        taps = scols[rows_at, :]
        totals = None
        for base in range(0, tokens, 256):
            q, terms = slopes(st, taps, rows_at, base, e[rows_at, pl.ds(base, 256)])
            squeue[rows_at, pl.ds(base, 256)] = q.astype(BF16)
            totals = terms if totals is None else [a + b for a, b in zip(totals, terms)]
        for k in range(5):
            acc[k, rows_at, :] = totals[k]

    sheads[...] = squeue[:, 0:128].astype(F32).T[0:8]

    @pl.when(zed > 0)
    def _():
        remote(sheads, shalo, halo_send.at[nz], halo_recv.at[nz], (dp, (zed - 1) * 2 + core))

    for k in range(5):
        line = jnp.sum(acc[k, 0:bc_rows].T, axis=0, keepdims=True)
        for z in range(nz):
            table_ref[z, 9 + k : 10 + k, 0 : 2 * sc] = line[:, z * 2 * sc : (z + 1) * 2 * sc]

    build_shifts(ahead, lambda k: 3 - k, 0)

    @pl.when(zed == nz - 1)
    def _():
        halo[...] = jnp.zeros(halo.shape, F32)
        shalo[...] = jnp.zeros(shalo.shape, F32)

    @pl.when(zed < nz - 1)
    def _():
        wait_for(shalo, halo_recv.at[nz])

    def back_taps(source, taps, rows_at, base):
        at = pl.ds(base, 256)
        grad = taps[:, 3:4] * source[rows_at, at].astype(F32)
        for k in range(3):
            grad = grad + taps[:, k : k + 1] * moved[k, rows_at, at].astype(F32)
        return grad

    squeue[:, tokens:] = jnp.concatenate([shalo[...], jnp.zeros((120, bc_rows), F32)], axis=0).T.astype(BF16)
    shift(squeue, bc_rows)
    for z in range(nz):
        for i in range(2 * sc // 16):
            rows_at = slice(z * 2 * sc + i * 16, z * 2 * sc + i * 16 + 16)
            mine = ((i * 16) // sc == core).astype(F32)
            taps = scols[rows_at, :] * mine
            for base in range(0, tokens, 256):
                slanes[z, i * 16 : i * 16 + 16, pl.ds(base, 256)] = back_taps(
                    squeue, taps, rows_at, base
                ).astype(BF16)
        slanes[z, 2 * sc : 2 * sc + 16, :] = jnp.concatenate(
            [steps_low[z * 8 : z * 8 + 8].astype(F32), jnp.zeros((8, tokens), F32)], axis=0
        ).astype(BF16)

    def values_back(z):
        @pl.when(zed < nz - 1)
        def _():
            wait_for(halo.at[z], halo_recv.at[z])

        queue[z, :, tokens:] = jnp.concatenate([halo[z], jnp.zeros((120, c), F32)], axis=0).T.astype(BF16)
        cols[...] = pars[2 * z + core, 0:8, :].T
        shift(queue.at[z], c)

        @pl.loop(0, c // 16, unroll=2)
        def _(i):
            rows_at = pl.ds(pl.multiple_of(i * 16, 16), 16)
            taps = cols[rows_at, :]
            for base in range(0, tokens, 256):
                turn[rows_at, pl.ds(base, 256)] = back_taps(queue.at[z], taps, rows_at, base).astype(BF16)

        vl[z] = turn[...].T

    @pl.loop(0, nz)
    def _(z):
        values_back(z)

    small_t[...] = slanes[...].reshape(nz * sr, tokens).T
    for i in range(2):
        wait_for(dstates.at[2 + i], ds_send.at[i])

    @pl.when(zed > 0)
    def _():
        for z in range(nz):
            wait_for(heads.at[z], halo_send.at[z])
        wait_for(sheads, halo_send.at[nz])


def conv_back(nz, sc, dx, p, db, dc, st, pars, match, ahead, v, dt, xdx, da, rates, mixed):
    inner, tokens = dx.shape
    c = inner // nz
    sr, most = 2 * sc + 16, max(c, st.shape[0])
    anywhere = pl.BlockSpec(memory_space=pl.ANY)
    vmem = pl.BlockSpec(memory_space=pltpu.VMEM)
    dma = pltpu.SemaphoreType.DMA

    def buffer(*dims, dtype=F32):
        return pltpu.VMEM(dims, dtype)

    low = functools.partial(buffer, dtype=BF16)
    return pl.pallas_call(
        functools.partial(conv_back_kernel, nz, sc),
        in_specs=[anywhere] * 5 + [vmem] * 9,
        out_specs=[vmem] * 3,
        out_shape=[shape((nz, tokens, c), BF16), shape((tokens, nz * sr), BF16), shape((nz, 16, c), F32)],
        scratch_shapes=[
            low(*st.shape), buffer(4, tokens, 128), buffer(most, tokens), low(c, LH + tokens), buffer(c, 8),
            buffer(st.shape[0], 5), low(tokens // 128, 256, 384), low(3, most, tokens), buffer(5, most, 128),
            low(nz, c, tokens + 128), low(st.shape[0], tokens + 128), buffer(nz, 8, c), buffer(nz, 8, c),
            buffer(8, st.shape[0]), buffer(8, st.shape[0]), low(c, tokens), low(nz, sr, tokens),
            dma((3,)), dma((2,)), dma((2,)), dma((2,)), dma((nz + 1,)), dma((nz + 1,)),
        ],
        compiler_params=pltpu.CompilerParams(
            collective_id=3, has_side_effects=True, vmem_limit_bytes=56 * MIB
        ),
        cost_estimate=cost(8 * inner * tokens * 384, 40 * MIB),
    )(dx, p, db, dc, st, pars, match, ahead, v, dt, xdx, da, rates, mixed)


def last_kernel(
    ndp, nz, sc,
    nt_hbm, vl_hbm, small_hbm, gl_hbm, wg_hbm, wv_hbm, ws_hbm, x_hbm, cot_hbm, planes, table_ref, gain_ref,
    sum_ref, grad_ref, norm_ref, row_ref, early_ref,
    nt, vl, small_t, gl, wg, wv, ws, x, cot, small_g, blocks, own, keep, send, got,
    got_first, got_second, got_hi, got_lo, z_out, z_got, tables, trows, norm_own, norms, norm_sum, norm_sums,
    load, w_load, first_send, first_recv, second_send, second_recv, hi_send, hi_recv, lo_send, lo_recv,
    z_send, z_recv, table_send, table_recv, trow_send, trow_recv, sib_send, sib_recv,
    norm_send, norm_recv, plane_send, plane_recv, early_send, early_recv, early_own,
):
    nh, lo = 2 * nz, ndp // 2
    width, tokens = nt.shape
    n = tokens // 2
    rows, c = own.shape[1:]
    sr = 2 * sc + 16
    r = width // ndp
    half = rows // 32 * 16
    dp, head = lax.axis_index("dp"), lax.axis_index("head")
    core, zed = lax.rem(head, 2), lax.div(head, 2)
    dhi, dlo = lax.div(dp, lo), lax.rem(dp, lo)
    hi_peer = (1 - dhi) * lo + dlo
    lo_peers = [dhi * lo + lax.rem(dlo + k, lo) for k in range(1, lo)]
    diagonal = [(1 - dhi) * lo + lax.rem(dlo + k, lo) for k in range(1, lo)]
    top, low = pl.ds(0, half), pl.ds(half, rows - half)
    order = [1] + [nz - 1] * (nz > 2) + list(range(2, nz - 1)) + [0]
    slots = [lax.rem(zed + zi, nz) for zi in order]

    loads = [
        pltpu.make_async_copy(a, b, load.at[i])
        for i, (a, b) in enumerate([
            (nt_hbm, nt), (small_hbm, small_t), (vl_hbm, vl), (gl_hbm, gl), (ws_hbm, ws), (x_hbm, x), (cot_hbm, cot),
        ])
    ]
    for copy in loads:
        copy.start()

    barrier = pltpu.get_barrier_semaphore()
    partners = [(dp, lax.rem(head + k, nh)) for k in range(1, nh)]
    partners += [(lax.rem(dp + k, ndp), head) for k in range(1, ndp)]
    for partner in partners:
        pl.semaphore_signal(barrier, inc=1, device_id=partner, device_id_type=MESH)
    pl.semaphore_wait(barrier, len(partners))

    def remote(src, dst, send_sem, recv_sem, device):
        pltpu.make_async_remote_copy(
            src_ref=src, dst_ref=dst, send_sem=send_sem, recv_sem=recv_sem, device_id=device, device_id_type=MESH
        ).start()

    def wait_for(ref, sem):
        pltpu.make_async_copy(ref, ref, sem).wait()

    for m in range(2):
        for k in range(1, nz):
            z = lax.rem(zed + k, nz)
            remote(
                planes.at[m, z], early_ref.at[m, zed], early_send.at[m, k], early_recv.at[m, zed], (dp, z * 2 + core)
            )
        pltpu.make_async_copy(planes.at[m, zed], early_ref.at[m, zed], early_own.at[m]).start()

    for k in range(1, ndp):
        remote(
            table_ref, tables.at[k - 1], table_send.at[k - 1], table_recv.at[k - 1], (lax.rem(dp + k, ndp), head)
        )

    def product(d, z, to):
        left = nt[pl.ds(pl.multiple_of(d * r, 16), r), :]
        to[0:r] = mm(left, vl[z], 1, 0).astype(to.dtype)
        at = pl.multiple_of(z * sr + core * sc, 16)
        to[r : r + sc] = small_g[d, pl.ds(at, sc), :].astype(to.dtype)
        to[r + sc : rows] = small_g[d, pl.ds(pl.multiple_of(z * sr + 2 * sc, 16), 16), :].astype(to.dtype)

    loads[0].wait()
    loads[1].wait()

    @pl.loop(0, ndp)
    def _(d):
        small_g[d] = mm(nt[pl.ds(pl.multiple_of(d * r, 16), r), :], small_t[...], 1, 0).T

    loads[2].wait()
    for j, z in enumerate(slots):
        for i, d in enumerate(diagonal):
            product(d, z, blocks.at[i, j])
            remote(
                blocks.at[i, j, top], got_first.at[i, z], first_send.at[i, j], first_recv.at[i, z],
                (lo_peers[i], head),
            )
            remote(
                blocks.at[i, j, low], got_second.at[i, z], second_send.at[i, j], second_recv.at[i, z],
                (hi_peer, head),
            )

    across = lo - 1
    for j, z in enumerate(slots):
        product(hi_peer, z, blocks.at[across, j])
        for i, d in enumerate(lo_peers):
            product(d, z, blocks.at[lo + i, j])
        product(dp, z, own.at[j])
        total = blocks[across, j, top].astype(F32)
        for i in range(lo - 1):
            wait_for(got_first.at[i, z], first_recv.at[i, z])
            total = total + got_first[i, z].astype(F32)
        blocks[across, j, top] = total.astype(BF16)
        remote(blocks.at[across, j], got_hi.at[z], hi_send.at[j], hi_recv.at[z], (hi_peer, head))
        for i, d in enumerate(lo_peers):
            wait_for(got_second.at[i, z], second_recv.at[i, z])
            blocks[lo + i, j, low] = (
                blocks[lo + i, j, low].astype(F32) + got_second[i, z].astype(F32)
            ).astype(BF16)
            remote(blocks.at[lo + i, j], got_lo.at[i, z], lo_send.at[i, j], lo_recv.at[i, z], (d, head))

    for copy in loads[3:5]:
        copy.wait()

    def weight_loads(d, slot):
        return [
            pltpu.make_async_copy(wg_hbm.at[d], wg.at[slot], w_load.at[0, slot]),
            pltpu.make_async_copy(wv_hbm.at[d], wv.at[slot], w_load.at[1, slot]),
        ]

    for copy in weight_loads(0, 0):
        copy.start()

    @pl.loop(0, ndp)
    def _(d):
        slot = lax.rem(d, 2)

        @pl.when(d < ndp - 1)
        def _():
            for copy in weight_loads(d + 1, 1 - slot):
                copy.start()

        for copy in weight_loads(d, slot):
            copy.wait()
        weights = [weight[slot].reshape(nz * c, r) for weight in (wg, wv)] + [ws[d].reshape(nz * sr, r)]
        for which, buffer in ((1 - core, send), (core, keep)):
            at = pl.ds(pl.multiple_of(which * n, 128), n)
            out = mm(small_t[at, :], weights[2], 1, 0)
            for left, weight in ((gl, weights[0]), (vl, weights[1])):
                out = out + mm(jnp.concatenate([left[z, at, :] for z in range(nz)], axis=1), weight, 1, 0)
            buffer[d] = out.astype(buffer.dtype)

    remote(send, got, sib_send.at[0], sib_recv.at[0], (dp, zed * 2 + 1 - core))

    def pass_on(j):
        z = slots[j]
        wait_for(got_hi.at[z], hi_recv.at[z])
        total = own[j] + got_hi[z].astype(F32)
        for i in range(lo - 1):
            wait_for(got_lo.at[i, z], lo_recv.at[i, z])
            total = total + got_lo[i, z].astype(F32)
        own[j] = total
        if order[j]:
            z_out[j] = total.astype(BF16)
            remote(z_out.at[j], z_got.at[zed], z_send.at[j], z_recv.at[zed], (dp, z * 2 + core))

    pass_on(0)

    total = table_ref[...]
    for k in range(1, ndp):
        wait_for(tables.at[k - 1], table_recv.at[k - 1])
        total = total + tables[k - 1]
    tables[ndp - 1] = total
    for j, z in enumerate(slots[:-1]):
        remote(tables.at[ndp - 1, z], trows.at[zed], trow_send.at[j], trow_recv.at[zed], (dp, z * 2 + core))

    for copy in loads[5:]:
        copy.wait()
    wait_for(got, sib_recv.at[0])
    norm_own[...] = jnp.zeros(norm_own.shape, F32)

    @pl.loop(0, n // 128)
    def _(i):
        at = pl.ds(pl.multiple_of(i * 128, 128), 128)
        full = jnp.concatenate([keep[d, at, :] + got[d, at, :].astype(F32) for d in range(ndp)], axis=1)
        tokens_x = x[at, :].astype(F32)
        inverse = lax.rsqrt(jnp.mean(tokens_x * tokens_x, axis=1, keepdims=True) + EPSILON)
        gained = full * gain_ref[...]
        dots = jnp.sum(gained * tokens_x, axis=1, keepdims=True)
        grad = inverse * gained - tokens_x * (inverse * inverse * inverse / width) * dots
        grad_ref[at, :] = (cot[at, :].astype(F32) + grad).astype(BF16)
        norm_own[0:1] += jnp.sum(full * (tokens_x * inverse), axis=0, keepdims=True)

    for k in range(1, nh):
        remote(
            norm_own, norms.at[k - 1], norm_send.at[k - 1], norm_recv.at[k - 1], (dp, lax.rem(head + k, nh))
        )
    for j in range(1, nz - 1):
        pass_on(j)
    total = norm_own[...]
    for k in range(1, nh):
        wait_for(norms.at[k - 1], norm_recv.at[k - 1])
        total = total + norms[k - 1]
    norm_sum[...] = total
    for k in range(1, ndp):
        remote(
            norm_sum, norm_sums.at[k - 1], plane_send.at[k - 1], plane_recv.at[k - 1],
            (lax.rem(dp + k, ndp), head),
        )
    pass_on(nz - 1)
    total = tables[ndp - 1, zed]
    for k in range(1, nz):
        z = lax.rem(zed + k, nz)
        wait_for(trows.at[z], trow_recv.at[z])
        total = total + trows[z]
    row_ref[...] = total
    total = norm_sum[...]
    for k in range(1, ndp):
        wait_for(norm_sums.at[k - 1], plane_recv.at[k - 1])
        total = total + norm_sums[k - 1]
    norm_ref[...] = total
    total = own[nz - 1]
    for k in range(1, nz):
        z = lax.rem(zed + k, nz)
        wait_for(z_got.at[z], z_recv.at[z])
        total = total + z_got[z].astype(F32)
    sum_ref[...] = total

    for m in range(2):
        pltpu.make_async_copy(planes.at[m, zed], early_ref.at[m, zed], early_own.at[m]).wait()
        for k in range(1, nz):
            z = lax.rem(zed + k, nz)
            wait_for(early_ref.at[m, z], early_recv.at[m, z])
            wait_for(planes.at[m, z], early_send.at[m, k])
    for j in range(nz):
        for i in range(lo - 1):
            wait_for(got_first.at[i, j], first_send.at[i, j])
            wait_for(got_second.at[i, j], second_send.at[i, j])
            wait_for(got_lo.at[i, j], lo_send.at[i, j])
        wait_for(got_hi.at[j], hi_send.at[j])
    for j in range(nz - 1):
        wait_for(z_out.at[j], z_send.at[j])
        wait_for(trows.at[j], trow_send.at[j])
    for k in range(ndp - 1):
        wait_for(table_ref, table_send.at[k])
        wait_for(norm_sum, plane_send.at[k])
    for k in range(nh - 1):
        wait_for(norm_own, norm_send.at[k])
    wait_for(send, sib_send.at[0])


def last_steps(ndp, nz, sc, nt, vl, small, gl, wg, wv, ws, x, cot, planes, table, gain):
    nh, lo = 2 * nz, ndp // 2
    width, tokens = nt.shape
    n = tokens // 2
    c = vl.shape[2]
    r = width // ndp
    rows = r + sc + 16
    half = rows // 32 * 16
    anywhere = pl.BlockSpec(memory_space=pl.ANY)
    vmem = pl.BlockSpec(memory_space=pltpu.VMEM)
    dma = pltpu.SemaphoreType.DMA

    def buffer(*dims, dtype=F32):
        return pltpu.VMEM(dims, dtype)

    low = functools.partial(buffer, dtype=BF16)
    return pl.pallas_call(
        functools.partial(last_kernel, ndp, nz, sc),
        in_specs=[anywhere] * 10 + [vmem] * 2,
        out_specs=[vmem] * 4 + [anywhere],
        out_shape=[
            shape((rows, c), F32),
            shape((n, width), BF16),
            shape((8, width), F32),
            shape((16, c), F32),
            shape(planes.shape, BF16),
        ],
        scratch_shapes=[
            low(width, tokens), low(*vl.shape), low(*small.shape), low(*gl.shape), low(2, nz, c, r), low(2, nz, c, r),
            low(*ws.shape), low(n, width), low(n, width), buffer(ndp, nz * ws.shape[2], r),
            low(ndp - 1, nz, rows, c), buffer(nz, rows, c), buffer(ndp, n, r), low(ndp, n, r), low(ndp, n, r),
            low(lo - 1, nz, half, c), low(lo - 1, nz, rows - half, c), low(nz, rows, c), low(lo - 1, nz, rows, c),
            low(nz - 1, rows, c), low(nz, rows, c), buffer(ndp, nz, 16, c), buffer(nz, 16, c),
            buffer(8, width), buffer(nh - 1, 8, width), buffer(8, width), buffer(ndp - 1, 8, width),
            dma((7,)), dma((2, 2)),
            dma((lo - 1, nz)), dma((lo - 1, nz)), dma((lo - 1, nz)), dma((lo - 1, nz)),
            dma((nz,)), dma((nz,)), dma((lo - 1, nz)), dma((lo - 1, nz)),
            dma((nz,)), dma((nz,)), dma((ndp - 1,)), dma((ndp - 1,)), dma((nz,)), dma((nz,)),
            dma((1,)), dma((1,)), dma((nh - 1,)), dma((nh - 1,)), dma((ndp - 1,)), dma((ndp - 1,)),
            dma((2, nz)), dma((2, nz)), dma((2,)),
        ],
        compiler_params=pltpu.CompilerParams(
            collective_id=2, has_side_effects=True, vmem_limit_bytes=63 * MIB
        ),
        cost_estimate=cost(4 * nz * c * tokens * width, 40 * MIB),
    )(nt, vl, small, gl, wg, wv, ws, x, cot, planes, table, gain)

def shards(
    block_input, lengths, norm_gain, in_gate, in_value, in_states, in_steps,
    conv_value, conv_value_bias, conv_states, conv_states_bias,
    step_bias, decay_log, skip_gain, gate_gain, out_proj, cotangent,
):
    ndp, nh = lax.axis_size("dp"), lax.axis_size("head")
    nz, lo = nh // 2, ndp // 2
    own, width = block_input.shape
    tokens = 2 * own
    dp, head = lax.axis_index("dp"), lax.axis_index("head")
    core, zed = head % 2, head // 2
    dhi, dlo = dp // lo, dp % lo
    r, cols = in_gate.shape
    hs, sc, taps = step_bias.shape[0], in_states.shape[1], conv_value.shape[0]
    heads, inner, state, hw = hs * nz, cols * nz, sc * nz, cols // hs
    total = 2 * inner

    def sibling(v):
        return lax.ppermute(v, "head", [(i, i ^ 1) for i in range(nh)])

    def zshift(v, k):
        return lax.ppermute(v, "head", [(i, (i + 2 * k) % nh) for i in range(nh)])

    def zstep(v, k):
        return lax.ppermute(
            v, "head", [(i, i + 2 * k) for i in range(nh) if 0 <= i + 2 * k < nh]
        )

    def lo_shift(v, k):
        return lax.ppermute(
            v, "dp", [(h * lo + i, h * lo + (i + k) % lo) for h in range(2) for i in range(lo)]
        )

    def hi_swap(v):
        return lax.ppermute(v, "dp", [(i, (i + lo) % ndp) for i in range(ndp)])

    def block(g, d, start, count):
        return lax.dynamic_slice(g, (d, 0, start, 0), (1, nz, count, g.shape[3]))[0]

    def slot(k):
        return (dlo + k) % lo

    def scatter_sends(g):
        rows = g.shape[2]
        half = rows // 32 * 16
        diagonal = [(1 - dhi) * lo + slot(k) for k in range(1, lo)]
        return [(block(g, d, 0, half), block(g, d, half, rows - half)) for d in diagonal]

    def scatter_first(sends):
        return [lo_shift(a, k + 1) for k, (a, _) in enumerate(sends)], [hi_swap(b) for _, b in sends]

    def scatter(g, first, second):
        rows = g.shape[2]
        half = rows // 32 * 16
        peer = (1 - dhi) * lo + dlo
        top = block(g, peer, 0, half).astype(F32)
        for v in first:
            top = top + v.astype(F32)
        sent = jnp.concatenate([top.astype(BF16), block(g, peer, half, rows - half)], axis=1)
        total_here = block(g, dp, 0, rows).astype(F32) + hi_swap(sent).astype(F32)
        for k in range(1, lo):
            d = dhi * lo + slot(k)
            low = block(g, d, half, rows - half).astype(F32) + second[k - 1].astype(F32)
            sent = jnp.concatenate([block(g, d, 0, half), low.astype(BF16)], axis=1)
            total_here = total_here + lo_shift(sent, k).astype(F32)
        return total_here.astype(BF16)

    heads_par = jnp.stack([step_bias, decay_log, skip_gain])
    (
        g_value, g_small, g_gate, g_out, everyone, normed_t, cot_t, value_pre, gate_pre, x_t, states_pre, bc,
        seg, match, ahead, v_steps, dt, a2, scale_back, rates, whole, sin,
    ) = gather_project(
        ndp, nz, sc, hs, hw, block_input, cotangent, in_value, in_gate, out_proj, in_states, in_steps,
        conv_value, conv_value_bias[None], gate_gain[None], heads_par, conv_states, conv_states_bias[None],
        norm_gain[None, :], lengths,
    )
    sin = sin.reshape(inner, state)
    x_t = x_t.reshape(inner, tokens)
    value_pre = value_pre.reshape(inner, LH + tokens)
    gate_pre = gate_pre.reshape(inner, tokens)
    bm, cm = bc[0], bc[1]
    places = [(i // hs) * 8 + i % hs for i in range(heads)]
    pars = lax.dynamic_index_in_dim(everyone.reshape(nz, 2, 16, cols), core, 1, keepdims=False)
    taps_t = pars[:, :8].transpose(0, 2, 1).reshape(inner, 8)
    gain = taps_t[:, 5:6]
    skip = pars[:, 8, :8].reshape(nz * 8)
    y_t, st = scan_forward(places, x_t, dt, a2, seg, bm, cm, sin, skip[:, None])

    gated, h1, sums = mix(g_out, cot_t, y_t, gate_pre, gain)
    sums = sums + sibling(sums)
    own_sums = lax.dynamic_slice_in_dim(sums, core * own, own, 1)
    out_blocks = weight_grad(ndp, cot_t, gated, sums=sums)
    out_sends = scatter_sends(out_blocks)
    y_late, out_sends = lax.optimization_barrier((y_t, out_sends))
    dy_t, gate_low, mix_cols, gate_blocks, rin = unmix(
        ndp, nz, hs, hw, y_late, gate_pre, h1, x_t, gain, sums, scale_back, cm, whole, normed_t
    )
    rin = rin.reshape(inner, state)
    plane_out = scatter(out_blocks, *scatter_first(out_sends))
    gate_first = scatter_first(scatter_sends(gate_blocks))
    dx_t, db, dc, xdx, da = scan_backward(
        places, x_t, dy_t, y_t, dt, a2, seg, bm, cm, st, rin, skip[:, None]
    )

    gate_first, dx_t = lax.optimization_barrier((gate_first, dx_t))
    plane_gate = scatter(gate_blocks, *gate_first)
    value_low, small_low, table = conv_back(
        nz, sc, dx_t, value_pre, db, dc, states_pre, everyone, match, ahead, v_steps, dt, xdx, da, rates, mix_cols
    )
    gated, table = lax.optimization_barrier((gated, table))
    keep, send = back_project(g_out, gated)
    out = result(total, keep, sibling(send), own_sums, block_input)
    sum_value, input_grad, norm_rows, row, early = last_steps(
        ndp, nz, sc, normed_t, value_low, small_low, gate_low, g_gate, g_value, g_small, block_input, cotangent,
        jnp.stack([plane_out, plane_gate]), table, norm_gain[None, :],
    )
    sum_out, sum_gate = early.astype(F32).sum(axis=1)
    own_lanes = lax.dynamic_slice_in_dim(row[6:14], zed * 8, hs, 1)
    states_row = lax.dynamic_slice_in_dim(row[9:14], core * sc, sc, 1)
    return (
        out,
        input_grad,
        norm_rows[0],
        sum_gate,
        sum_value[:r],
        sum_value[r : r + sc].T,
        sum_value[r + sc : r + sc + hs].T,
        row[:taps],
        row[4],
        states_row[:taps],
        states_row[taps],
        own_lanes[0],
        own_lanes[1],
        row[8].reshape(hs, hw).sum(axis=1),
        row[5],
        sum_out,
    )


def solution(mesh):
    both = P(("dp", "head"), None)
    grid = P("dp", "head")
    return jax.shard_map(
        shards,
        mesh=mesh,
        in_specs=(
            both, P("dp", None), P(), grid, grid, grid, grid,
            P(None, "head"), P("head"), P(None, "head"), P("head"),
            P("head"), P("head"), P("head"), P("head"), grid, both,
        ),
        out_specs=(
            both, both, P(), grid, grid, grid, grid,
            P(None, "head"), P("head"), P(None, "head"), P("head"),
            P("head"), P("head"), P("head"), P("head"), grid,
        ),
        check_vma=False,
    )
```

time: 2460 us -> 494 us (0.20)
  waiting for transfers between devices: 915 us -> 1.23 us
  local copies, waits for them, and re-layouts: 606 us -> 33.9 us
  matrix products: 456 us -> 0 us
  Pallas kernels: 0 us -> 428 us
  other arithmetic: 344 us -> 19.7 us
  blocking collectives: 61.3 us -> 0 us
  loops' own time: 45.7 us -> 0 us
    dot_general x239 -> x0, matrix products: 456 us -> none  [the longest x48 104 us: advance(): jnp.einsum('tsh,shp->thp', scores[:, :, None] * weights, driven, precisio...]
    pallas_call x0 -> x10, Pallas kernels: none -> 428 us  [the longest x1 154 us: gather_project(): pl.pallas_call(functools.partial(gather_kernel, ndp, nz, sc, hs, hw), in_...]
    psum x1 -> x0, waiting for transfers between devices: 419 us -> none  [shards(): full_grad = lax.psum(normed_grad, 'head')]
    reduce_scatter x7 -> x0, waiting for transfers between devices: 385 us -> none  [the longest x1 213 us: shards(): lax.psum_scatter(partial_branch, 'head', scatter_dimension=0, tiled=True)]
    dynamic_update_slice x80 -> x0, local copies, waits for them, and re-layouts: 331 us -> none  [state_space(): _, result = lax.scan(jax.checkpoint(advance), start, pieces)]
    another operation x146 -> x4, other arithmetic: 184 us -> 8.63 us  [the longest x3 7.35 us: shards(): jnp.stack([plane_out, plane_gate])]
    all_gather x6 -> x0, waiting for transfers between devices: 108 us -> none  [the longest x1 108 us: shards(): gathered = lax.all_gather(block_input, 'head', axis=0, tiled=True)]
    convert_element_type x41 -> x2, other arithmetic: 73.2 us -> 3.59 us  [scatter(): top.astype(BF16)]
  transfers between devices with their start and end apart: 14 -> 10, of which waited for: 8 -> 1; matrix products, arithmetic and copies ran while one was open for 26% -> 7% of each run, Pallas kernels for 0% -> 47%
where the time goes in v1:
time: 494 us; the launch traced here: 493 us
  Pallas kernels  428 us (87%)
  local copies, waits for them, and re-layouts  33.9 us (7%)
  other arithmetic  19.7 us (4%)
  starting transfers between devices  8.23 us (2%)
    pallas_call x1, Pallas kernels, gather_project(): pl.pallas_call(functools.partial(gather_kernel, ndp, nz, sc, hs, hw), in_...  154 us
    pallas_call x1, Pallas kernels, last_steps(): pl.pallas_call(functools.partial(last_kernel, ndp, nz, sc), in_specs=[any...  97.3 us
    pallas_call x1, Pallas kernels, conv_back(): pl.pallas_call(functools.partial(conv_back_kernel, nz, sc), in_specs=[any...  54.8 us
    pallas_call x1, Pallas kernels, unmix(): pl.pallas_call(functools.partial(unmix_kernel, ndp, nz, hs, hw, inner * 2...  44.5 us
    pallas_call x1, Pallas kernels, scan_backward(): pl.pallas_call(functools.partial(scan_bwd_kernel, places, inner // len(pl...  23.8 us
    pallas_call x1, Pallas kernels, mix(): pl.pallas_call(functools.partial(mix_kernel, ndp), grid=(nz,), in_specs=[...  16.3 us
    pallas_call x1, Pallas kernels, scan_forward(): pl.pallas_call(functools.partial(scan_fwd_kernel, places, inner // len(pl...  13.7 us
    pallas_call x1, Pallas kernels, weight_grad(): pl.pallas_call(functools.partial(weight_grad_kernel, ndp, 0 if sums is No...  10 us
  transfers between devices with their start and end apart: 10, of which 1 were waited for; matrix products, arithmetic and copies ran while one was open for 7% of the time, Pallas kernels for 47%

profile of v1, /device:TPU:0, one launch (start us, length us, event | category | flops | bytes accessed | tf_op | source)
XLA Modules:
  0.0 492.6 jit_solution(9311422373701161626)
XLA Ops:
  2.0 1.5 copy.33.states_ref
  3.4 1.5 copy.34.stepw_ref
  8.7 153.5 %shard_map.288 = (bf16[4,4,384,384]{3,2,1,0:T(8,128)(2,1)}, bf16[4,4,80,384]{3,2,1,0:T(8,128)(2,1)}, bf16[4,4,384,384]{3,2,1,0:T(8,128)(2,1)}, bf16[4,4,384,384]...) custom-call(bf16[512,1536]{1,0:T(8,128)(2,1)} %x_hbm.1, ...), custom_call_target="tpu_custom_call" | custom-call | flops 11274289152 | bytes 62914560 | tf_op jit(solution)/shard_map/pallas_call | solution.py:703
  165.1 13.7 %shard_map.289 = (f32[1536,1024]{1,0:T(8,128)}, bf16[8,1536,128]{2,1,0:T(8,128)(2,1)S(1)}) custom-call(bf16[1536,1024]{1,0:T(8,128)(2,1)} %bitcast.74, f32[32,1024]{1,0:T(8,128)S(1)} %copy-done.15, f32[32,1024]{1,0:T(8,128)S(1)} %copy-done.18, f32[8,1152]{1,0:T(8,128)S(1)} %copy-done.19, bf16[1024,128]{1,0:T(8,128)(2,1)S(1)} %get-tuple-element.144.b_ref, ...), custom_call_target="tpu_custom_call" | custom-call | flops 4026531840 | bytes 15728640 | tf_op jit(solution)/shard_map/pallas_call | solution.py:192
  178.7 1.6 copy-done.12
  180.4 16.3 %shard_map.290 = (bf16[4,1024,384]{2,1,0:T(8,128)(2,1)S(1)}, f32[1536,1024]{1,0:T(8,128)}, f32[8,1024]{1,0:T(8,128)S(1)}) custom-call(bf16[4,4,384,384]{3,2,1,0:T(8,128)(2,1)} %get-tuple-element.71.wo_ref.weight_ref, bf16[1536,1024]{1,0:T(8,128)(2,1)} %get-tuple-element.72.ct_ref.refs_0_, f32[1536,1024]{1,0:T(8,128)} %get-tuple-element.84.y_ref, ...), custom_call_target="tpu_custom_call" | custom-call | flops 4831838208 | bytes 34603008 | tf_op jit(solution)/shard_map/pallas_call | solution.py:823
  196.7 1.7 copy-done.9
  199.6 1.9 copy-done.3
  201.5 10.0 %shard_map.291 = bf16[4,4,384,384]{3,2,1,0:T(8,128)(2,1)} custom-call(bf16[1536,1024]{1,0:T(8,128)(2,1)S(1)} %copy-done.3, bf16[4,1024,384]{2,1,0:T(8,128)(2,1)} %copy-done.9, f32[8,1024]{1,0:T(8,128)S(1)} %add.97.refs_2_.sums_ref), custom_call_target="tpu_custom_call" | custom-call | flops 4831838208 | bytes 12582912 | tf_op jit(solution)/shard_map/pallas_call | solution.py:1035
  211.5 2.9 dynamic-slice_bitcast_fusion.3
  216.4 44.5 %shard_map.292 = (bf16[1536,1024]{1,0:T(8,128)(2,1)}, bf16[4,1024,384]{2,1,0:T(8,128)(2,1)}, f32[4,8,384]{2,1,0:T(8,128)}, bf16[4,4,384,384]{3,2,1,0:T(8,128)(2,1)}, bf16[4,384,128]{2,1,0:T(8,128)(2,1)}) custom-call(f32[1536,1024]{1,0:T(8,128)} %get-tuple-element.84.y_ref, f32[1536,1024]{1,0:T(8,128)} %bitcast.80, f32[1536,1024]{1,0:T(8,128)} %get-tuple-element.85.h1_ref, ...), custom_call_target="tpu_custom_call" | custom-call | flops 5234491392 | bytes 44040192 | tf_op jit(solution)/shard_map/pallas_call | solution.py:970
  261.0 2.0 dynamic-slice_bitcast_fusion.1
  263.3 1.7 collective-permute-start.2
  265.1 23.8 %shard_map.293 = (f32[1536,1024]{1,0:T(8,128)}, f32[1024,128]{1,0:T(8,128)S(1)}, f32[1024,128]{1,0:T(8,128)S(1)}, f32[32,1024]{1,0:T(8,128)S(1)}, f32[32,1024]{1,0:T(8,128)S(1)}) custom-call(bf16[1536,1024]{1,0:T(8,128)(2,1)S(1)} %bitcast.76, bf16[1536,1024]{1,0:T(8,128)(2,1)} %get-tuple-element.90.dy_ref, f32[1536,1024]{1,0:T(8,128)} %get-tuple-element.84.y_ref, ...), custom_call_target="tpu_custom_call" | custom-call | flops 12079595520 | bytes 25165824 | tf_op jit(solution)/shard_map/pallas_call | solution.py:214
  289.0 2.1 fusion.9
  293.8 1.7 collective-permute-start.7
  295.5 1.5 fusion.7
  299.6 1.7 collective-permute-start.9
  301.3 54.8 %shard_map.294 = (bf16[4,1024,384]{2,1,0:T(8,128)(2,1)}, bf16[1024,320]{1,0:T(8,128)(2,1)}, f32[4,16,384]{2,1,0:T(8,128)}) custom-call(f32[1536,1024]{1,0:T(8,128)} %get-tuple-element.94.dx_hbm, bf16[1536,1152]{1,0:T(8,128)(2,1)} %bitcast.91, f32[1024,128]{1,0:T(8,128)} %copy-done.13, f32[1024,128]{1,0:T(8,128)} %copy-done.14, ...), custom_call_target="tpu_custom_call" | custom-call | flops 4831838208 | bytes 41943040 | tf_op jit(solution)/shard_map/pallas_call | solution.py:1351
  356.2 9.8 %shard_map.295 = (f32[4,512,384]{2,1,0:T(8,128)S(1)}, bf16[4,512,384]{2,1,0:T(8,128)(2,1)}) custom-call(bf16[4,4,384,384]{3,2,1,0:T(8,128)(2,1)} %get-tuple-element.71.wo_ref.weight_ref, bf16[4,1024,384]{2,1,0:T(8,128)(2,1)} %copy-done.9), custom_call_target="tpu_custom_call" | custom-call | flops 4831838208 | bytes 3145728 | tf_op jit(solution)/shard_map/pallas_call | solution.py:1063
  366.0 3.2 fusion.4
  369.3 2.4 fusion.5
  371.7 1.7 pad_maximum_fusion.planes
  373.4 97.3 %shard_map.297 = (f32[432,384]{1,0:T(8,128)}, bf16[512,1536]{1,0:T(8,128)(2,1)}, f32[8,1536]{1,0:T(8,128)}, f32[16,384]{1,0:T(8,128)}, bf16[2,4,384,384]{3,2,1,0:T(8,128)(2,1)}) custom-call(bf16[1536,1024]{1,0:T(8,128)(2,1)} %get-tuple-element.88.nt_ref.nt_hbm, bf16[4,1024,384]{2,1,0:T(8,128)(2,1)} %get-tuple-element.110.vl_hbm, ...), custom_call_target="tpu_custom_call" | custom-call | flops 9663676416 | bytes 41943040 | tf_op jit(solution)/shard_map/pallas_call | solution.py:1626
  472.2 1.4 slice_reduce_fusion.1
  473.6 1.3 slice.66
  474.9 1.9 slice.63
  478.2 1.4 slice_reduce_fusion
  480.7 1.3 slice_bitcast_fusion.6
  482.0 1.4 slice_bitcast_fusion.5
  483.4 2.2 convert_reduce_fusion
  486.8 4.7 shard_map.296
  (92 shorter events, 22.9 us)
Async XLA Ops:
  162.2 2.8 copy-start.11
  162.2 2.8 copy-start.15
  162.2 2.8 copy-start.18
  162.3 2.8 copy-start.19
  164.4 14.3 %copy-start.5 = (bf16[1024,128]{1,0:T(8,128)(2,1)}, bf16[1024,128]{1,0:T(8,128)(2,1)S(1)}, u32[]{:S(2)}) copy-start(bf16[1024,128]{1,0:T(8,128)(2,1)S(1)} %get-tuple-element.143.c_ref.cm_ref) | copy-start | bytes 786436
  165.0 15.4 %copy-start = (f32[1536,1]{1,0:T(8,128)}, f32[1536,1]{1,0:T(8,128)S(1)}, u32[]{:S(2)}) copy-start(f32[1536,1]{1,0:T(8,128)S(1)} %slice.78.gain_ref) | copy-start | bytes 18436
  198.4 1.2 collective-permute-start
  199.6 11.9 %copy-start.7 = (f32[8,1024]{1,0:T(8,128)}, f32[8,1024]{1,0:T(8,128)S(1)}, u32[]{:S(2)}) copy-start(f32[8,1024]{1,0:T(8,128)S(1)} %add.97.refs_2_.sums_ref) | copy-start | bytes 98308
  199.6 1.9 copy-start.3
  214.4 74.5 %collective-permute-start.4 = (bf16[4,192,384]{2,1,0:T(8,128)(2,1)}, bf16[4,192,384]{2,1,0:T(8,128)(2,1)}, u32[]{:S(2)}, u32[]{:S(2)}) collective-permute-start(bf16[4,192,384]{2,1,0:T(8,128)(2,1)} %get-tuple-element.116), channel_id=1, source_target_pairs={{0,8},{8,0},{16,24},{24,16},{1,9},{9,1},{17,25},{25,17},{2,10},{10... | collective-permute-start | bytes 1769480 | tf_op jit(solution)/shard_map/ppermute | solution.py:1686
  215.6 73.4 %collective-permute-start.6 = (bf16[4,192,384]{2,1,0:T(8,128)(2,1)}, bf16[4,192,384]{2,1,0:T(8,128)(2,1)}, u32[]{:S(2)}, u32[]{:S(2)}) collective-permute-start(bf16[4,192,384]{2,1,0:T(8,128)(2,1)} %get-tuple-element.117), channel_id=1, source_target_pairs={{0,16},{8,24},{16,0},{24,8},{1,17},{9,25},{17,1},{25,9},{2,18},{10... | collective-permute-start | bytes 1769480 | tf_op jit(solution)/shard_map/ppermute | solution.py:1691
  260.9 4.1 copy-start.2
  260.9 4.1 copy-start.6
  260.9 4.1 copy-start.10
  260.9 28.0 %slice-start = ((s8[4718592]{0:T(1024)(128)(4,1)}), s8[4194304]{0:T(1024)(128)(4,1)S(1)}, s32[]{:S(2)}) async-start(s8[4718592]{0:T(1024)(128)(4,1)} %bitcast.81), calls=%async_computation | async-start | bytes 8388608
  263.0 32.6 %collective-permute-start.1 = (bf16[4,192,384]{2,1,0:T(8,128)(2,1)S(1)}, bf16[4,192,384]{2,1,0:T(8,128)(2,1)S(1)}, u32[]{:S(2)}, u32[]{:S(2)}) collective-permute-start(bf16[4,192,384]{2,1,0:T(8,128)(2,1)S(1)} %get-tuple-element.140), channel_id=1, source_target_pairs={{0,8},{8,0},{16,24},{24,16},{1,9},{9,1},{17,25},{25,17},{2,10},{10... | collective-permute-start | bytes 1769480 | tf_op jit(solution)/shard_map/ppermute | solution.py:1686
  263.3 32.2 %collective-permute-start.2 = (bf16[4,192,384]{2,1,0:T(8,128)(2,1)S(1)}, bf16[4,192,384]{2,1,0:T(8,128)(2,1)S(1)}, u32[]{:S(2)}, u32[]{:S(2)}) collective-permute-start(bf16[4,192,384]{2,1,0:T(8,128)(2,1)S(1)} %get-tuple-element.139), channel_id=1, source_target_pairs={{0,16},{8,24},{16,0},{24,8},{1,17},{9,25},{17,1},{25,9},{2,18},{10... | collective-permute-start | bytes 1769480 | tf_op jit(solution)/shard_map/ppermute | solution.py:1691
  265.0 23.8 %copy-start.8 = (f32[8,1024]{1,0:T(8,128)S(1)}, f32[8,1024]{1,0:T(8,128)}, u32[]{:S(2)}) copy-start(f32[8,1024]{1,0:T(8,128)} %copy-done.7) | copy-start | bytes 98308
  265.1 23.9 %slice-start.1 = ((s8[4718592]{0:T(1024)(128)(4,1)}), s8[524288]{0:T(1024)(128)(4,1)S(1)}, s32[]{:S(2)}) async-start(s8[4718592]{0:T(1024)(128)(4,1)} %bitcast.81), calls=%async_computation.1 | async-start | bytes 1048576
  288.9 3.3 copy-start.13
  288.9 3.3 copy-start.14
  288.9 3.3 copy-start.16
  288.9 3.3 copy-start.17
  288.9 2.1 copy-start.20
  292.2 73.8 %collective-permute-start.5 = (bf16[4,384,384]{2,1,0:T(8,128)(2,1)}, bf16[4,384,384]{2,1,0:T(8,128)(2,1)}, u32[]{:S(2)}, u32[]{:S(2)}) collective-permute-start(bf16[4,384,384]{2,1,0:T(8,128)(2,1)} %pad_maximum_fusion.1), channel_id=1, source_target_pairs={{0,16},{8,24},{16,0},{24,8},{1,17},{9,25},{17,1},{25,9},{2,18},{10... | collective-permute-start | bytes 3538952 | tf_op jit(solution)/shard_map/ppermute | solution.py:1691
  293.8 72.2 %collective-permute-start.7 = (bf16[4,384,384]{2,1,0:T(8,128)(2,1)}, bf16[4,384,384]{2,1,0:T(8,128)(2,1)}, u32[]{:S(2)}, u32[]{:S(2)}) collective-permute-start(bf16[4,384,384]{2,1,0:T(8,128)(2,1)} %pad_maximum_fusion.2), channel_id=1, source_target_pairs={{0,8},{8,0},{16,24},{24,16},{1,9},{9,1},{17,25},{25,17},{2,10},{10... | collective-permute-start | bytes 3538952 | tf_op jit(solution)/shard_map/ppermute | solution.py:1686
  298.2 71.0 %collective-permute-start.8 = (bf16[4,384,384]{2,1,0:T(8,128)(2,1)}, bf16[4,384,384]{2,1,0:T(8,128)(2,1)}, u32[]{:S(2)}, u32[]{:S(2)}) collective-permute-start(bf16[4,384,384]{2,1,0:T(8,128)(2,1)} %pad_maximum_fusion.3), channel_id=1, source_target_pairs={{0,16},{8,24},{16,0},{24,8},{1,17},{9,25},{17,1},{25,9},{2,18},{10... | collective-permute-start | bytes 3538952 | tf_op jit(solution)/shard_map/ppermute | solution.py:1691
  299.6 69.6 %collective-permute-start.9 = (bf16[4,384,384]{2,1,0:T(8,128)(2,1)}, bf16[4,384,384]{2,1,0:T(8,128)(2,1)}, u32[]{:S(2)}, u32[]{:S(2)}) collective-permute-start(bf16[4,384,384]{2,1,0:T(8,128)(2,1)} %pad_maximum_fusion.4), channel_id=1, source_target_pairs={{0,8},{8,0},{16,24},{24,16},{1,9},{9,1},{17,25},{25,17},{2,10},{10... | collective-permute-start | bytes 3538952 | tf_op jit(solution)/shard_map/ppermute | solution.py:1686
  366.0 3.2 copy-start.1
  366.0 120.7 %collective-permute-start.3 = (bf16[4,512,384]{2,1,0:T(8,128)(2,1)}, bf16[4,512,384]{2,1,0:T(8,128)(2,1)}, u32[]{:S(2)}, u32[]{:S(2)}) collective-permute-start(bf16[4,512,384]{2,1,0:T(8,128)(2,1)} %get-tuple-element.109), channel_id=1, source_target_pairs={{0,1},{1,0},{2,3},{3,2},{4,5},{5,4},{6,7},{7,6},{8,9},{9,8},{10,11... | collective-permute-start | bytes 4718600 | tf_op jit(solution)/shard_map/ppermute | solution.py:1675
  483.4 3.3 copy-start.4
  486.8 4.7 copy-start.21
  (2 other events, 3.3 us)

commit v2 on v1

--- a/solution.py
+++ b/solution.py
@@ -1044,66 +1044,13 @@
     )(*operands)
 
 
-def back_project_kernel(nz, n, weight_ref, right_ref, keep_ref, send_ref):
-    core = lax.rem(lax.axis_index("head"), 2)
-    weight = jnp.concatenate([weight_ref[0, z] for z in range(nz)], axis=0)
-
-    def product(which):
-        at = pl.ds(pl.multiple_of(which * n, 128), n)
-        return mm(jnp.concatenate([right_ref[z, at, :] for z in range(nz)], axis=1), weight, 1, 0)
-
-    send_ref[0] = product(1 - core).astype(BF16)
-    keep_ref[0] = product(core)
-
-
-def back_project(weight, right):
-    ndp, nz, c, r = weight.shape
-    tokens = right.shape[1]
-    n = tokens // 2
-    return pl.pallas_call(
-        functools.partial(back_project_kernel, nz, n),
-        grid=(ndp,),
-        in_specs=[
-            pl.BlockSpec((1, nz, c, r), lambda d: (d, 0, 0, 0)),
-            pl.BlockSpec(right.shape, lambda d: (0, 0, 0)),
-        ],
-        out_specs=[pl.BlockSpec((1, n, r), lambda d: (d, 0, 0))] * 2,
-        out_shape=[shape((ndp, n, r), F32), shape((ndp, n, r), BF16)],
-        compiler_params=params(),
-        cost_estimate=cost(2 * weight.size * tokens, 2 * right.size),
-    )(weight, right)
-
-
-def result_kernel(total, keep_ref, got_ref, sums_ref, x_ref, out_ref):
-    inverse = lax.rsqrt(sums_ref[...].T[:, 0:1] / total + EPSILON)
-    blocks = [keep_ref[d] + got_ref[d].astype(F32) for d in range(keep_ref.shape[0])]
-    branch = jnp.concatenate(blocks, axis=1)
-    out_ref[...] = (x_ref[...].astype(F32) + branch * inverse).astype(BF16)
-
-
-def result(total, keep, got, sums, x):
-    n, width = x.shape
-    ndp, _, r = keep.shape
-    blocks = pl.BlockSpec((ndp, 128, r), lambda i: (0, i, 0))
-    rows = pl.BlockSpec((128, width), lambda i: (i, 0))
-    return pl.pallas_call(
-        functools.partial(result_kernel, total),
-        grid=(n // 128,),
-        in_specs=[blocks, blocks, pl.BlockSpec((8, 128), lambda i: (0, i)), rows],
-        out_specs=rows,
-        out_shape=shape((n, width), BF16),
-        compiler_params=params(),
-        cost_estimate=cost(0, 12 * n * width),
-    )(keep, got, sums, x)
-
-
 def conv_back_kernel(
     nz, sc,
-    dx_hbm, p_hbm, db_hbm, dc_hbm, st_hbm,
+    dx_hbm, p_hbm, db_hbm, dc_hbm, st_hbm, plane,
     pars, match, ahead, v_ref, dt_ref, xdx_ref, da_ref, rates_ref, mix_ref,
-    vl, small_t, table_ref,
+    vl, small_t, table_ref, early_ref,
     st, dstates, e, p, cols, scols, shifts, moved, acc, queue, squeue, heads, halo, sheads, shalo, turn, slanes,
-    load, e_load, ds_send, ds_recv, halo_send, halo_recv,
+    load, e_load, ds_send, ds_recv, halo_send, halo_recv, early_send, early_recv, early_own,
 ):
     nh = 2 * nz
     _, c, wide = queue.shape
@@ -1143,6 +1090,12 @@
 
     for i, ref in enumerate((db_hbm, dc_hbm)):
         remote(ref, dstates.at[2 + i], ds_send.at[i], ds_recv.at[i], (dp, zed * 2 + 1 - core))
+
+    for k in range(1, nz):
+        z = lax.rem(zed + k, nz)
+        remote(plane.at[z], early_ref.at[zed], early_send.at[k], early_recv.at[zed], (dp, z * 2 + core))
+    keep_own = pltpu.make_async_copy(plane.at[zed], early_ref.at[zed], early_own.at[0])
+    keep_own.start()
 
     place = lax.broadcasted_iota(jnp.int32, (256, 128), 0) - lax.broadcasted_iota(jnp.int32, (256, 128), 1)
 
@@ -1326,6 +1279,11 @@
         values_back(z)
 
     small_t[...] = slanes[...].reshape(nz * sr, tokens).T
+    keep_own.wait()
+    for k in range(1, nz):
+        z = lax.rem(zed + k, nz)
+        wait_for(early_ref.at[z], early_recv.at[z])
+        wait_for(plane.at[z], early_send.at[k])
     for i in range(2):
         wait_for(dstates.at[2 + i], ds_send.at[i])
 
@@ -1336,7 +1294,7 @@
         wait_for(sheads, halo_send.at[nz])
 
 
-def conv_back(nz, sc, dx, p, db, dc, st, pars, match, ahead, v, dt, xdx, da, rates, mixed):
+def conv_back(nz, sc, dx, p, db, dc, st, plane, pars, match, ahead, v, dt, xdx, da, rates, mixed):
     inner, tokens = dx.shape
     c = inner // nz
     sr, most = 2 * sc + 16, max(c, st.shape[0])
@@ -1350,31 +1308,34 @@
     low = functools.partial(buffer, dtype=BF16)
     return pl.pallas_call(
         functools.partial(conv_back_kernel, nz, sc),
-        in_specs=[anywhere] * 5 + [vmem] * 9,
-        out_specs=[vmem] * 3,
-        out_shape=[shape((nz, tokens, c), BF16), shape((tokens, nz * sr), BF16), shape((nz, 16, c), F32)],
+        in_specs=[anywhere] * 6 + [vmem] * 9,
+        out_specs=[vmem] * 3 + [anywhere],
+        out_shape=[shape((nz, tokens, c), BF16), shape((tokens, nz * sr), BF16), shape((nz, 16, c), F32), shape(plane.shape, BF16)],
         scratch_shapes=[
             low(*st.shape), buffer(4, tokens, 128), buffer(most, tokens), low(c, LH + tokens), buffer(c, 8),
             buffer(st.shape[0], 5), low(tokens // 128, 256, 384), low(3, most, tokens), buffer(5, most, 128),
             low(nz, c, tokens + 128), low(st.shape[0], tokens + 128), buffer(nz, 8, c), buffer(nz, 8, c),
             buffer(8, st.shape[0]), buffer(8, st.shape[0]), low(c, tokens), low(nz, sr, tokens),
-            dma((3,)), dma((2,)), dma((2,)), dma((2,)), dma((nz + 1,)), dma((nz + 1,)),
+            dma((3,)), dma((2,)), dma((2,)), dma((2,)), dma((nz + 1,)), dma((nz + 1,)), dma((nz,)), dma((nz,)), dma((1,)),
         ],
         compiler_params=pltpu.CompilerParams(
             collective_id=3, has_side_effects=True, vmem_limit_bytes=56 * MIB
         ),
         cost_estimate=cost(8 * inner * tokens * 384, 40 * MIB),
-    )(dx, p, db, dc, st, pars, match, ahead, v, dt, xdx, da, rates, mixed)
+    )(dx, p, db, dc, st, plane, pars, match, ahead, v, dt, xdx, da, rates, mixed)
 
 
 def last_kernel(
     ndp, nz, sc,
-    nt_hbm, vl_hbm, small_hbm, gl_hbm, wg_hbm, wv_hbm, ws_hbm, x_hbm, cot_hbm, planes, table_ref, gain_ref,
-    sum_ref, grad_ref, norm_ref, row_ref, early_ref,
+    nt_hbm, vl_hbm, small_hbm, gl_hbm, wg_hbm, wv_hbm, ws_hbm, x_hbm, cot_hbm, plane, gated_hbm, wo_hbm,
+    table_ref, gain_ref, sums_ref,
+    sum_ref, grad_ref, norm_ref, row_ref, out_ref, early_ref,
     nt, vl, small_t, gl, wg, wv, ws, x, cot, small_g, blocks, own, keep, send, got,
+    keep_out, send_out, got_out,
     got_first, got_second, got_hi, got_lo, z_out, z_got, tables, trows, norm_own, norms, norm_sum, norm_sums,
     load, w_load, first_send, first_recv, second_send, second_recv, hi_send, hi_recv, lo_send, lo_recv,
     z_send, z_recv, table_send, table_recv, trow_send, trow_recv, sib_send, sib_recv,
+    out_send, out_recv, gated_load,
     norm_send, norm_recv, plane_send, plane_recv, early_send, early_recv, early_own,
 ):
     nh, lo = 2 * nz, ndp // 2
@@ -1418,13 +1379,11 @@
     def wait_for(ref, sem):
         pltpu.make_async_copy(ref, ref, sem).wait()
 
-    for m in range(2):
-        for k in range(1, nz):
-            z = lax.rem(zed + k, nz)
-            remote(
-                planes.at[m, z], early_ref.at[m, zed], early_send.at[m, k], early_recv.at[m, zed], (dp, z * 2 + core)
-            )
-        pltpu.make_async_copy(planes.at[m, zed], early_ref.at[m, zed], early_own.at[m]).start()
+    for k in range(1, nz):
+        z = lax.rem(zed + k, nz)
+        remote(plane.at[z], early_ref.at[zed], early_send.at[k], early_recv.at[zed], (dp, z * 2 + core))
+    keep_own = pltpu.make_async_copy(plane.at[zed], early_ref.at[zed], early_own.at[0])
+    keep_own.start()
 
     for k in range(1, ndp):
         remote(
@@ -1522,7 +1481,33 @@
             z_out[j] = total.astype(BF16)
             remote(z_out.at[j], z_got.at[zed], z_send.at[j], z_recv.at[zed], (dp, z * 2 + core))
 
+    get_gated = pltpu.make_async_copy(gated_hbm, gl, gated_load.at[0])
+    get_gated.start()
+
+    def out_loads(d, slot):
+        return pltpu.make_async_copy(wo_hbm.at[d], wg.at[slot], w_load.at[0, slot])
+
+    out_loads(0, 0).start()
     pass_on(0)
+    get_gated.wait()
+
+    @pl.loop(0, ndp)
+    def _(d):
+        slot = lax.rem(d, 2)
+
+        @pl.when(d < ndp - 1)
+        def _():
+            out_loads(d + 1, 1 - slot).start()
+
+        out_loads(d, slot).wait()
+        weight = wg[slot].reshape(nz * c, r)
+        for which, buffer in ((1 - core, send_out), (core, keep_out)):
+            at = pl.ds(pl.multiple_of(which * n, 128), n)
+            left = jnp.concatenate([gl[z, at, :] for z in range(nz)], axis=1)
+            buffer[d] = mm(left, weight, 1, 0).astype(buffer.dtype)
+
+    remote(send_out, got_out, out_send.at[0], out_recv.at[0], (dp, zed * 2 + 1 - core))
+    pass_on(1)
 
     total = table_ref[...]
     for k in range(1, ndp):
@@ -1553,7 +1538,7 @@
         remote(
             norm_own, norms.at[k - 1], norm_send.at[k - 1], norm_recv.at[k - 1], (dp, lax.rem(head + k, nh))
         )
-    for j in range(1, nz - 1):
+    for j in range(2, nz - 1):
         pass_on(j)
     total = norm_own[...]
     for k in range(1, nh):
@@ -1565,6 +1550,15 @@
             norm_sum, norm_sums.at[k - 1], plane_send.at[k - 1], plane_recv.at[k - 1],
             (lax.rem(dp + k, ndp), head),
         )
+    wait_for(got_out, out_recv.at[0])
+
+    @pl.loop(0, n // 128)
+    def _(i):
+        at = pl.ds(pl.multiple_of(i * 128, 128), 128)
+        inverse = lax.rsqrt(sums_ref[:, at].T[:, 0:1] / (2 * nz * c) + EPSILON)
+        branch = jnp.concatenate([keep_out[d, at, :] + got_out[d, at, :].astype(F32) for d in range(ndp)], axis=1)
+        out_ref[at, :] = (x[at, :].astype(F32) + branch * inverse).astype(BF16)
+
     pass_on(nz - 1)
     total = tables[ndp - 1, zed]
     for k in range(1, nz):
@@ -1584,12 +1578,11 @@
         total = total + z_got[z].astype(F32)
     sum_ref[...] = total
 
-    for m in range(2):
-        pltpu.make_async_copy(planes.at[m, zed], early_ref.at[m, zed], early_own.at[m]).wait()
-        for k in range(1, nz):
-            z = lax.rem(zed + k, nz)
-            wait_for(early_ref.at[m, z], early_recv.at[m, z])
-            wait_for(planes.at[m, z], early_send.at[m, k])
+    keep_own.wait()
+    for k in range(1, nz):
+        z = lax.rem(zed + k, nz)
+        wait_for(early_ref.at[z], early_recv.at[z])
+        wait_for(plane.at[z], early_send.at[k])
     for j in range(nz):
         for i in range(lo - 1):
             wait_for(got_first.at[i, j], first_send.at[i, j])
@@ -1605,9 +1598,10 @@
     for k in range(nh - 1):
         wait_for(norm_own, norm_send.at[k])
     wait_for(send, sib_send.at[0])
-
-
-def last_steps(ndp, nz, sc, nt, vl, small, gl, wg, wv, ws, x, cot, planes, table, gain):
+    wait_for(send_out, out_send.at[0])
+
+
+def last_steps(ndp, nz, sc, nt, vl, small, gl, wg, wv, ws, x, cot, plane, gated, wo, table, gain, sums):
     nh, lo = 2 * nz, ndp // 2
     width, tokens = nt.shape
     n = tokens // 2
@@ -1625,19 +1619,21 @@
     low = functools.partial(buffer, dtype=BF16)
     return pl.pallas_call(
         functools.partial(last_kernel, ndp, nz, sc),
-        in_specs=[anywhere] * 10 + [vmem] * 2,
-        out_specs=[vmem] * 4 + [anywhere],
+        in_specs=[anywhere] * 12 + [vmem] * 3,
+        out_specs=[vmem] * 5 + [anywhere],
         out_shape=[
             shape((rows, c), F32),
             shape((n, width), BF16),
             shape((8, width), F32),
             shape((16, c), F32),
-            shape(planes.shape, BF16),
+            shape((n, width), BF16),
+            shape(plane.shape, BF16),
         ],
         scratch_shapes=[
             low(width, tokens), low(*vl.shape), low(*small.shape), low(*gl.shape), low(2, nz, c, r), low(2, nz, c, r),
             low(*ws.shape), low(n, width), low(n, width), buffer(ndp, nz * ws.shape[2], r),
             low(ndp - 1, nz, rows, c), buffer(nz, rows, c), buffer(ndp, n, r), low(ndp, n, r), low(ndp, n, r),
+            buffer(ndp, n, r), low(ndp, n, r), low(ndp, n, r),
             low(lo - 1, nz, half, c), low(lo - 1, nz, rows - half, c), low(nz, rows, c), low(lo - 1, nz, rows, c),
             low(nz - 1, rows, c), low(nz, rows, c), buffer(ndp, nz, 16, c), buffer(nz, 16, c),
             buffer(8, width), buffer(nh - 1, 8, width), buffer(8, width), buffer(ndp - 1, 8, width),
@@ -1645,14 +1641,14 @@
             dma((lo - 1, nz)), dma((lo - 1, nz)), dma((lo - 1, nz)), dma((lo - 1, nz)),
             dma((nz,)), dma((nz,)), dma((lo - 1, nz)), dma((lo - 1, nz)),
             dma((nz,)), dma((nz,)), dma((ndp - 1,)), dma((ndp - 1,)), dma((nz,)), dma((nz,)),
-            dma((1,)), dma((1,)), dma((nh - 1,)), dma((nh - 1,)), dma((ndp - 1,)), dma((ndp - 1,)),
-            dma((2, nz)), dma((2, nz)), dma((2,)),
+            dma((1,)), dma((1,)), dma((1,)), dma((1,)), dma((1,)), dma((nh - 1,)), dma((nh - 1,)), dma((ndp - 1,)), dma((ndp - 1,)),
+            dma((nz,)), dma((nz,)), dma((1,)),
         ],
         compiler_params=pltpu.CompilerParams(
             collective_id=2, has_side_effects=True, vmem_limit_bytes=63 * MIB
         ),
         cost_estimate=cost(4 * nz * c * tokens * width, 40 * MIB),
-    )(nt, vl, small, gl, wg, wv, ws, x, cot, planes, table, gain)
+    )(nt, vl, small, gl, wg, wv, ws, x, cot, plane, gated, wo, table, gain, sums)
 
 def shards(
     block_input, lengths, norm_gain, in_gate, in_value, in_states, in_steps,
@@ -1705,21 +1701,24 @@
     def scatter_first(sends):
         return [lo_shift(a, k + 1) for k, (a, _) in enumerate(sends)], [hi_swap(b) for _, b in sends]
 
-    def scatter(g, first, second):
+    def scatter(g, first, second, hold=None):
         rows = g.shape[2]
         half = rows // 32 * 16
         peer = (1 - dhi) * lo + dlo
         top = block(g, peer, 0, half).astype(F32)
         for v in first:
             top = top + v.astype(F32)
-        sent = jnp.concatenate([top.astype(BF16), block(g, peer, half, rows - half)], axis=1)
-        total_here = block(g, dp, 0, rows).astype(F32) + hi_swap(sent).astype(F32)
+        sents = [jnp.concatenate([top.astype(BF16), block(g, peer, half, rows - half)], axis=1)]
         for k in range(1, lo):
             d = dhi * lo + slot(k)
             low = block(g, d, half, rows - half).astype(F32) + second[k - 1].astype(F32)
-            sent = jnp.concatenate([block(g, d, 0, half), low.astype(BF16)], axis=1)
-            total_here = total_here + lo_shift(sent, k).astype(F32)
-        return total_here.astype(BF16)
+            sents.append(jnp.concatenate([block(g, d, 0, half), low.astype(BF16)], axis=1))
+        if hold is not None:
+            sents, hold = lax.optimization_barrier((sents, hold))
+        total_here = block(g, dp, 0, rows).astype(F32) + hi_swap(sents[0]).astype(F32)
+        for k in range(1, lo):
+            total_here = total_here + lo_shift(sents[k], k).astype(F32)
+        return total_here.astype(BF16), hold
 
     heads_par = jnp.stack([step_bias, decay_log, skip_gain])
     (
@@ -1752,25 +1751,23 @@
         ndp, nz, hs, hw, y_late, gate_pre, h1, x_t, gain, sums, scale_back, cm, whole, normed_t
     )
     rin = rin.reshape(inner, state)
-    plane_out = scatter(out_blocks, *scatter_first(out_sends))
     gate_first = scatter_first(scatter_sends(gate_blocks))
+    plane_out, dy_t = scatter(out_blocks, *scatter_first(out_sends), hold=dy_t)
     dx_t, db, dc, xdx, da = scan_backward(
         places, x_t, dy_t, y_t, dt, a2, seg, bm, cm, st, rin, skip[:, None]
     )
 
     gate_first, dx_t = lax.optimization_barrier((gate_first, dx_t))
-    plane_gate = scatter(gate_blocks, *gate_first)
-    value_low, small_low, table = conv_back(
-        nz, sc, dx_t, value_pre, db, dc, states_pre, everyone, match, ahead, v_steps, dt, xdx, da, rates, mix_cols
+    plane_gate, _ = scatter(gate_blocks, *gate_first)
+    value_low, small_low, table, early_out = conv_back(
+        nz, sc, dx_t, value_pre, db, dc, states_pre, plane_out, everyone, match, ahead, v_steps, dt, xdx, da, rates, mix_cols
     )
-    gated, table = lax.optimization_barrier((gated, table))
-    keep, send = back_project(g_out, gated)
-    out = result(total, keep, sibling(send), own_sums, block_input)
-    sum_value, input_grad, norm_rows, row, early = last_steps(
+    sum_value, input_grad, norm_rows, row, out, early_gate = last_steps(
         ndp, nz, sc, normed_t, value_low, small_low, gate_low, g_gate, g_value, g_small, block_input, cotangent,
-        jnp.stack([plane_out, plane_gate]), table, norm_gain[None, :],
+        plane_gate, gated, g_out, table, norm_gain[None, :], own_sums,
     )
-    sum_out, sum_gate = early.astype(F32).sum(axis=1)
+    sum_out = early_out.astype(F32).sum(axis=0)
+    sum_gate = early_gate.astype(F32).sum(axis=0)
     own_lanes = lax.dynamic_slice_in_dim(row[6:14], zed * 8, hs, 1)
     states_row = lax.dynamic_slice_in_dim(row[9:14], core * sc, sc, 1)
     return (

time: 494 us -> 472 us (0.955)
  Pallas kernels: 428 us -> 404 us
    pallas_call x2 -> x0, Pallas kernels: 14.5 us -> none  [the longest x1 9.84 us: back_project(): pl.pallas_call(functools.partial(back_project_kernel, nz, n), grid=(ndp,)...]
    pallas_call x1, Pallas kernels: 97.3 us -> 87.7 us  [last_steps(): pl.pallas_call(functools.partial(last_kernel, ndp, nz, sc), in_specs=[any...]
    convert_element_type x0 -> x3, other arithmetic: none -> 7.77 us  [the longest x2 6.21 us: scatter(): return (total_here.astype(BF16), hold)]
    another operation x3 -> x0, other arithmetic: 7.35 us -> none  [shards(): jnp.stack([plane_out, plane_gate])]
    unnamed x51 -> x48, local copies, waits for them, and re-layouts: 9.42 us -> 11.3 us
  transfers between devices with their start and end apart: 10 -> 9, of which waited for: 1 -> 2; matrix products, arithmetic and copies ran while one was open for 7% -> 3% of each run, Pallas kernels for 47% -> 26%
where the time goes in v2:
time: 472 us; the launch traced here: 471 us
  Pallas kernels  404 us (86%)
  local copies, waits for them, and re-layouts  34.4 us (7%)
  other arithmetic  17.5 us (4%)
  starting transfers between devices  8.24 us (2%)
  waiting for transfers between devices  5.09 us (1%)
    pallas_call x1, Pallas kernels, gather_project(): pl.pallas_call(functools.partial(gather_kernel, ndp, nz, sc, hs, hw), in_...  154 us
    pallas_call x1, Pallas kernels, last_steps(): pl.pallas_call(functools.partial(last_kernel, ndp, nz, sc), in_specs=[any...  87.7 us
    pallas_call x1, Pallas kernels, conv_back(): pl.pallas_call(functools.partial(conv_back_kernel, nz, sc), in_specs=[any...  54.9 us
    pallas_call x1, Pallas kernels, unmix(): pl.pallas_call(functools.partial(unmix_kernel, ndp, nz, hs, hw, inner * 2...  44.4 us
    pallas_call x1, Pallas kernels, scan_backward(): pl.pallas_call(functools.partial(scan_bwd_kernel, places, inner // len(pl...  23.8 us
    pallas_call x1, Pallas kernels, mix(): pl.pallas_call(functools.partial(mix_kernel, ndp), grid=(nz,), in_specs=[...  16.3 us
    pallas_call x1, Pallas kernels, scan_forward(): pl.pallas_call(functools.partial(scan_fwd_kernel, places, inner // len(pl...  13.5 us
    unnamed x48, local copies, waits for them, and re-layouts  11.3 us
  transfers between devices with their start and end apart: 9, of which 2 were waited for; matrix products, arithmetic and copies ran while one was open for 3% of the time, Pallas kernels for 26%

profile of v2, /device:TPU:0, one launch (start us, length us, event | category | flops | bytes accessed | tf_op | source)
XLA Modules:
  0.0 470.5 jit_solution(11011368986651825293)
XLA Ops:
  0.7 1.3 broadcast_in_dim.16.gain_ref
  2.0 1.5 copy.33.states_ref
  3.4 1.5 copy.34.stepw_ref
  7.4 1.3 pad_maximum_fusion.4.heads_ref
  8.7 153.6 %shard_map.288 = (bf16[4,4,384,384]{3,2,1,0:T(8,128)(2,1)}, bf16[4,4,80,384]{3,2,1,0:T(8,128)(2,1)}, bf16[4,4,384,384]{3,2,1,0:T(8,128)(2,1)}, bf16[4,4,384,384]...) custom-call(bf16[512,1536]{1,0:T(8,128)(2,1)} %x_hbm.1, ...), custom_call_target="tpu_custom_call" | custom-call | flops 11274289152 | bytes 62914560 | tf_op jit(solution)/shard_map/pallas_call | solution.py:703
  165.1 13.5 %shard_map.289 = (f32[1536,1024]{1,0:T(8,128)}, bf16[8,1536,128]{2,1,0:T(8,128)(2,1)S(1)}) custom-call(bf16[1536,1024]{1,0:T(8,128)(2,1)} %bitcast.66, f32[32,1024]{1,0:T(8,128)S(1)} %copy-done.13, f32[32,1024]{1,0:T(8,128)S(1)} %copy-done.16, f32[8,1152]{1,0:T(8,128)S(1)} %copy-done.17, bf16[1024,128]{1,0:T(8,128)(2,1)S(1)} %get-tuple-element.144.b_ref, ...), custom_call_target="tpu_custom_call" | custom-call | flops 4026531840 | bytes 15728640 | tf_op jit(solution)/shard_map/pallas_call | solution.py:192
  178.6 1.7 copy-done.10
  180.3 16.3 %shard_map.290 = (bf16[4,1024,384]{2,1,0:T(8,128)(2,1)S(1)}, f32[1536,1024]{1,0:T(8,128)}, f32[8,1024]{1,0:T(8,128)S(1)}) custom-call(bf16[4,4,384,384]{3,2,1,0:T(8,128)(2,1)} %get-tuple-element.82.wo_ref.wo_hbm, bf16[1536,1024]{1,0:T(8,128)(2,1)} %get-tuple-element.81.ct_ref.refs_0_, f32[1536,1024]{1,0:T(8,128)} %get-tuple-element.86.y_ref, ...), custom_call_target="tpu_custom_call" | custom-call | flops 4831838208 | bytes 34603008 | tf_op jit(solution)/shard_map/pallas_call | solution.py:823
  196.6 1.6 copy-done.7
  199.4 1.9 copy-done.2
  201.3 10.0 %shard_map.291 = bf16[4,4,384,384]{3,2,1,0:T(8,128)(2,1)} custom-call(bf16[1536,1024]{1,0:T(8,128)(2,1)S(1)} %copy-done.2, bf16[4,1024,384]{2,1,0:T(8,128)(2,1)} %copy-done.7, f32[8,1024]{1,0:T(8,128)S(1)} %add.97.refs_2_.sums_ref), custom_call_target="tpu_custom_call" | custom-call | flops 4831838208 | bytes 12582912 | tf_op jit(solution)/shard_map/pallas_call | solution.py:1035
  211.4 1.9 dynamic-slice_bitcast_fusion.2
  215.4 44.4 %shard_map.292 = (bf16[1536,1024]{1,0:T(8,128)(2,1)}, bf16[4,1024,384]{2,1,0:T(8,128)(2,1)}, f32[4,8,384]{2,1,0:T(8,128)}, bf16[4,4,384,384]{3,2,1,0:T(8,128)(2,1)}, bf16[4,384,128]{2,1,0:T(8,128)(2,1)}) custom-call(f32[1536,1024]{1,0:T(8,128)} %get-tuple-element.86.y_ref, f32[1536,1024]{1,0:T(8,128)} %bitcast.72, f32[1536,1024]{1,0:T(8,128)} %get-tuple-element.87.h1_ref, ...), custom_call_target="tpu_custom_call" | custom-call | flops 5234491392 | bytes 44040192 | tf_op jit(solution)/shard_map/pallas_call | solution.py:970
  259.8 1.9 dynamic-slice_bitcast_fusion.1
  262.2 1.6 collective-permute-start.2
  263.8 1.6 fusion.6
  265.4 1.6 pad_maximum_fusion
  267.4 1.7 collective-permute-start.6
  269.1 23.8 %shard_map.293 = (f32[1536,1024]{1,0:T(8,128)}, f32[1024,128]{1,0:T(8,128)S(1)}, f32[1024,128]{1,0:T(8,128)S(1)}, f32[32,1024]{1,0:T(8,128)S(1)}, f32[32,1024]{1,0:T(8,128)S(1)}) custom-call(bf16[1536,1024]{1,0:T(8,128)(2,1)S(1)} %bitcast.68, bf16[1536,1024]{1,0:T(8,128)(2,1)} %get-tuple-element.94.dy_ref, f32[1536,1024]{1,0:T(8,128)} %get-tuple-element.86.y_ref, ...), custom_call_target="tpu_custom_call" | custom-call | flops 12079595520 | bytes 25165824 | tf_op jit(solution)/shard_map/pallas_call | solution.py:214
  293.0 2.0 fusion.5
  297.6 1.7 collective-permute-start.8
  299.9 3.9 collective-permute-done.5
  303.7 2.8 fusion.3.plane
  306.5 54.9 %shard_map.294 = (bf16[4,1024,384]{2,1,0:T(8,128)(2,1)}, bf16[1024,320]{1,0:T(8,128)(2,1)}, f32[4,16,384]{2,1,0:T(8,128)}, bf16[4,384,384]{2,1,0:T(8,128)(2,1)}) custom-call(f32[1536,1024]{1,0:T(8,128)} %get-tuple-element.98.dx_hbm, bf16[1536,1152]{1,0:T(8,128)(2,1)} %bitcast.81, f32[1024,128]{1,0:T(8,128)} %copy-done.11, f32[1024,128]{1,0:T(8,128)} %copy-done.12, ...), custom_call_target="tpu_custom_call" | custom-call | flops 4831838208 | bytes 41943040 | tf_op jit(solution)/shard_map/pallas_call | solution.py:1309
  361.4 3.5 fusion.1.plane
  364.9 87.7 %shard_map.295 = (f32[432,384]{1,0:T(8,128)}, bf16[512,1536]{1,0:T(8,128)(2,1)}, f32[8,1536]{1,0:T(8,128)}, f32[16,384]{1,0:T(8,128)}, bf16[512,1536]{1,0:T(8,128)(2,1)}, /*index=5*/bf16[4,384,384]{2,1,0:T(8,128)(2,1)}) custom-call(bf16[1536,1024]{1,0:T(8,128)(2,1)} %get-tuple-element.72.nt_ref.nt_hbm, bf16[4,1024,384]{2,1,0:T(8,128)(2,1)} %get-tuple-element.112.vl_hbm, ...), custom_call_target="tpu_custom_call" | custom-call | flops 9663676416 | bytes 41943040 | tf_op jit(solution)/shard_map/pallas_call | solution.py:1620
  455.3 2.0 slice.63
  457.3 1.4 slice_bitcast_fusion.3
  458.8 1.3 slice_bitcast_fusion.4
  460.1 1.4 slice_reduce_fusion.1
  461.5 1.3 slice.66
  464.4 1.4 slice_reduce_fusion
  (82 shorter events, 21.7 us)
Async XLA Ops:
  163.3 1.7 copy-start.9
  163.3 1.7 copy-start.13
  163.3 1.7 copy-start.16
  163.3 1.8 copy-start.17
  164.5 14.2 %copy-start.3 = (bf16[1024,128]{1,0:T(8,128)(2,1)}, bf16[1024,128]{1,0:T(8,128)(2,1)S(1)}, u32[]{:S(2)}) copy-start(bf16[1024,128]{1,0:T(8,128)(2,1)S(1)} %get-tuple-element.143.c_ref.cm_ref) | copy-start | bytes 786436
  165.0 15.3 %copy-start = (f32[1536,1]{1,0:T(8,128)}, f32[1536,1]{1,0:T(8,128)S(1)}, u32[]{:S(2)}) copy-start(f32[1536,1]{1,0:T(8,128)S(1)} %slice.78.gain_ref) | copy-start | bytes 18436
  178.6 1.7 copy-start.10
  196.6 1.6 copy-start.7
  198.2 1.2 collective-permute-start
  199.4 11.9 %copy-start.5 = (f32[8,1024]{1,0:T(8,128)}, f32[8,1024]{1,0:T(8,128)S(1)}, u32[]{:S(2)}) copy-start(f32[8,1024]{1,0:T(8,128)S(1)} %add.97.refs_2_.sums_ref) | copy-start | bytes 98308
  199.4 1.9 copy-start.2
  213.3 50.6 %collective-permute-start.3 = (bf16[4,192,384]{2,1,0:T(8,128)(2,1)S(1)}, bf16[4,192,384]{2,1,0:T(8,128)(2,1)S(1)}, u32[]{:S(2)}, u32[]{:S(2)}) collective-permute-start(bf16[4,192,384]{2,1,0:T(8,128)(2,1)S(1)} %get-tuple-element.91), channel_id=1, source_target_pairs={{0,8},{8,0},{16,24},{24,16},{1,9},{9,1},{17,25},{25,17},{2,10},{10... | collective-permute-start | bytes 1769480 | tf_op jit(solution)/shard_map/ppermute | solution.py:1682
  214.5 49.3 %collective-permute-start.4 = (bf16[4,192,384]{2,1,0:T(8,128)(2,1)S(1)}, bf16[4,192,384]{2,1,0:T(8,128)(2,1)S(1)}, u32[]{:S(2)}, u32[]{:S(2)}) collective-permute-start(bf16[4,192,384]{2,1,0:T(8,128)(2,1)S(1)} %get-tuple-element.92), channel_id=1, source_target_pairs={{0,16},{8,24},{16,0},{24,8},{1,17},{9,25},{17,1},{25,9},{2,18},{10... | collective-permute-start | bytes 1769480 | tf_op jit(solution)/shard_map/ppermute | solution.py:1687
  261.8 31.2 %collective-permute-start.1 = (bf16[4,192,384]{2,1,0:T(8,128)(2,1)S(1)}, bf16[4,192,384]{2,1,0:T(8,128)(2,1)S(1)}, u32[]{:S(2)}, u32[]{:S(2)}) collective-permute-start(bf16[4,192,384]{2,1,0:T(8,128)(2,1)S(1)} %get-tuple-element.136), channel_id=1, source_target_pairs={{0,8},{8,0},{16,24},{24,16},{1,9},{9,1},{17,25},{25,17},{2,10},{10... | collective-permute-start | bytes 1769480 | tf_op jit(solution)/shard_map/ppermute | solution.py:1682
  262.2 30.8 %collective-permute-start.2 = (bf16[4,192,384]{2,1,0:T(8,128)(2,1)S(1)}, bf16[4,192,384]{2,1,0:T(8,128)(2,1)S(1)}, u32[]{:S(2)}, u32[]{:S(2)}) collective-permute-start(bf16[4,192,384]{2,1,0:T(8,128)(2,1)S(1)} %get-tuple-element.135), channel_id=1, source_target_pairs={{0,16},{8,24},{16,0},{24,8},{1,17},{9,25},{17,1},{25,9},{2,18},{10... | collective-permute-start | bytes 1769480 | tf_op jit(solution)/shard_map/ppermute | solution.py:1687
  265.4 3.7 copy-start.1
  265.4 3.7 copy-start.4
  265.4 3.7 copy-start.8
  267.1 36.7 %collective-permute-start.5 = (bf16[4,384,384]{2,1,0:T(8,128)(2,1)}, bf16[4,384,384]{2,1,0:T(8,128)(2,1)S(1)}, u32[]{:S(2)}, u32[]{:S(2)}) collective-permute-start(bf16[4,384,384]{2,1,0:T(8,128)(2,1)} %get-tuple-element.103), channel_id=1, source_target_pairs={{0,16},{8,24},{16,0},{24,8},{1,17},{9,25},{17,1},{25,9},{2,18},{10... | collective-permute-start | bytes 3538952 | tf_op jit(solution)/shard_map/ppermute | solution.py:1687
  267.4 36.3 %collective-permute-start.6 = (bf16[4,384,384]{2,1,0:T(8,128)(2,1)}, bf16[4,384,384]{2,1,0:T(8,128)(2,1)S(1)}, u32[]{:S(2)}, u32[]{:S(2)}) collective-permute-start(bf16[4,384,384]{2,1,0:T(8,128)(2,1)} %get-tuple-element.104), channel_id=1, source_target_pairs={{0,8},{8,0},{16,24},{24,16},{1,9},{9,1},{17,25},{25,17},{2,10},{10... | collective-permute-start | bytes 3538952 | tf_op jit(solution)/shard_map/ppermute | solution.py:1682
  292.9 2.0 copy-start.11
  292.9 2.0 copy-start.12
  292.9 2.0 copy-start.14
  292.9 2.0 copy-start.15
  296.1 3.1 copy-start.6
  296.1 65.3 %collective-permute-start.7 = (bf16[4,384,384]{2,1,0:T(8,128)(2,1)}, bf16[4,384,384]{2,1,0:T(8,128)(2,1)}, u32[]{:S(2)}, u32[]{:S(2)}) collective-permute-start(bf16[4,384,384]{2,1,0:T(8,128)(2,1)} %pad_maximum_fusion.2), channel_id=1, source_target_pairs={{0,16},{8,24},{16,0},{24,8},{1,17},{9,25},{17,1},{25,9},{2,18},{10... | collective-permute-start | bytes 3538952 | tf_op jit(solution)/shard_map/ppermute | solution.py:1687
  297.6 63.9 %collective-permute-start.8 = (bf16[4,384,384]{2,1,0:T(8,128)(2,1)}, bf16[4,384,384]{2,1,0:T(8,128)(2,1)}, u32[]{:S(2)}, u32[]{:S(2)}) collective-permute-start(bf16[4,384,384]{2,1,0:T(8,128)(2,1)} %pad_maximum_fusion.3), channel_id=1, source_target_pairs={{0,8},{8,0},{16,24},{24,16},{1,9},{9,1},{17,25},{25,17},{2,10},{10... | collective-permute-start | bytes 3538952 | tf_op jit(solution)/shard_map/ppermute | solution.py:1682
  452.6 10.2 %copy-start.21 = (bf16[4,384,384]{2,1,0:T(8,128)(2,1)S(1)}, bf16[4,384,384]{2,1,0:T(8,128)(2,1)}, u32[]{:S(2)}) copy-start(bf16[4,384,384]{2,1,0:T(8,128)(2,1)} %get-tuple-element.124) | copy-start | bytes 3538948
  455.3 10.5 %copy-start.20 = (bf16[4,384,384]{2,1,0:T(8,128)(2,1)S(1)}, bf16[4,384,384]{2,1,0:T(8,128)(2,1)}, u32[]{:S(2)}) copy-start(bf16[4,384,384]{2,1,0:T(8,128)(2,1)} %get-tuple-element.127) | copy-start | bytes 3538948
  462.8 4.7 copy-start.19
  467.4 2.0 copy-start.18

commit v3 on v2

--- a/solution.py
+++ b/solution.py
@@ -326,8 +326,12 @@
     wv_ref[...] = wv_in[...].T
     along_z(0, wv_ref, gv_ref.at[dp, zed])
     near(0, gv_ref, 0, wv_ref)
-    small_t = pltpu.roll(lanes(states_ref[...], 0), core * sc, 1) + lanes(stepw_ref[...], 2 * sc)
-    ws_ref[...] = small_t.T[0 : ws_ref.shape[0]].astype(BF16)
+    own_states = states_ref[...].astype(F32)
+    first_core = (core == 0).astype(F32)
+    ws_ref[...] = jnp.concatenate(
+        [own_states * first_core, own_states * (1.0 - first_core), stepw_ref[...].astype(F32),
+         jnp.zeros((16 - hs, r), F32)], axis=0,
+    ).astype(BF16)
     remote(ws_ref, small_sib, misc_send.at[0], misc_recv.at[0], (dp, sib))
     own_rows = pl.ds(HALO + core * n, n)
     remote(x_ref, xbuf.at[own_rows], misc_send.at[1], misc_recv.at[1], (dp, sib))
@@ -1049,7 +1053,7 @@
     dx_hbm, p_hbm, db_hbm, dc_hbm, st_hbm, plane,
     pars, match, ahead, v_ref, dt_ref, xdx_ref, da_ref, rates_ref, mix_ref,
     vl, small_t, table_ref, early_ref,
-    st, dstates, e, p, cols, scols, shifts, moved, acc, queue, squeue, heads, halo, sheads, shalo, turn, slanes,
+    st, dstates, e2, p2, cols, scols, shifts, moved, acc, queue, squeue, heads, halo, sheads, shalo, turn, slanes,
     load, e_load, ds_send, ds_recv, halo_send, halo_recv, early_send, early_recv, early_own,
 ):
     nh = 2 * nz
@@ -1060,10 +1064,10 @@
     core, zed = lax.rem(head, 2), lax.div(head, 2)
 
     def column_loads(z):
-        at = pl.ds(pl.multiple_of(z * c, 16), c)
+        at, place = pl.ds(pl.multiple_of(z * c, 16), c), lax.rem(z, 2)
         return [
-            pltpu.make_async_copy(dx_hbm.at[at], e.at[pl.ds(0, c)], e_load.at[0]),
-            pltpu.make_async_copy(p_hbm.at[at], p, e_load.at[1]),
+            pltpu.make_async_copy(dx_hbm.at[at], e2.at[place, pl.ds(0, c)], e_load.at[0, place]),
+            pltpu.make_async_copy(p_hbm.at[at], p2.at[place], e_load.at[1, place]),
         ]
 
     for copy in column_loads(0):
@@ -1135,8 +1139,14 @@
 
     @pl.loop(0, nz)
     def _(z):
+        @pl.when(z < nz - 1)
+        def _():
+            for copy in column_loads(z + 1):
+                copy.start()
+
         for copy in column_loads(z):
             copy.wait()
+        e, p = e2.at[lax.rem(z, 2)], p2.at[lax.rem(z, 2)]
         cols[...] = pars[2 * z + core, 0:8, :].T
         shift(p, c)
 
@@ -1151,11 +1161,6 @@
                 totals = terms if totals is None else [a + b for a, b in zip(totals, terms)]
             for k in range(5):
                 acc[k, rows_at, :] = totals[k]
-
-        @pl.when(z < nz - 1)
-        def _():
-            for copy in column_loads(z + 1):
-                copy.start()
 
         heads[z] = queue[z, :, 0:128].astype(F32).T[0:8]
 
@@ -1195,7 +1200,7 @@
     def _(b):
         at = pl.ds(pl.multiple_of(b * 128, 128), 128)
         for i in range(2):
-            e[i * 128 : i * 128 + 128, at] = (dstates[i, at, :] + dstates[2 + i, at, :]).T
+            e2[0, i * 128 : i * 128 + 128, at] = (dstates[i, at, :] + dstates[2 + i, at, :]).T
 
     bc_rows = 2 * sc * nz
     shift(st, bc_rows)
@@ -1206,7 +1211,7 @@
         taps = scols[rows_at, :]
         totals = None
         for base in range(0, tokens, 256):
-            q, terms = slopes(st, taps, rows_at, base, e[rows_at, pl.ds(base, 256)])
+            q, terms = slopes(st, taps, rows_at, base, e2[0, rows_at, pl.ds(base, 256)])
             squeue[rows_at, pl.ds(base, 256)] = q.astype(BF16)
             totals = terms if totals is None else [a + b for a, b in zip(totals, terms)]
         for k in range(5):
@@ -1312,11 +1317,11 @@
         out_specs=[vmem] * 3 + [anywhere],
         out_shape=[shape((nz, tokens, c), BF16), shape((tokens, nz * sr), BF16), shape((nz, 16, c), F32), shape(plane.shape, BF16)],
         scratch_shapes=[
-            low(*st.shape), buffer(4, tokens, 128), buffer(most, tokens), low(c, LH + tokens), buffer(c, 8),
+            low(*st.shape), buffer(4, tokens, 128), buffer(2, most, tokens), low(2, c, LH + tokens), buffer(c, 8),
             buffer(st.shape[0], 5), low(tokens // 128, 256, 384), low(3, most, tokens), buffer(5, most, 128),
             low(nz, c, tokens + 128), low(st.shape[0], tokens + 128), buffer(nz, 8, c), buffer(nz, 8, c),
             buffer(8, st.shape[0]), buffer(8, st.shape[0]), low(c, tokens), low(nz, sr, tokens),
-            dma((3,)), dma((2,)), dma((2,)), dma((2,)), dma((nz + 1,)), dma((nz + 1,)), dma((nz,)), dma((nz,)), dma((1,)),
+            dma((3,)), dma((2, 2)), dma((2,)), dma((2,)), dma((nz + 1,)), dma((nz + 1,)), dma((nz,)), dma((nz,)), dma((1,)),
         ],
         compiler_params=pltpu.CompilerParams(
             collective_id=3, has_side_effects=True, vmem_limit_bytes=56 * MIB
@@ -1725,7 +1730,7 @@
         g_value, g_small, g_gate, g_out, everyone, normed_t, cot_t, value_pre, gate_pre, x_t, states_pre, bc,
         seg, match, ahead, v_steps, dt, a2, scale_back, rates, whole, sin,
     ) = gather_project(
-        ndp, nz, sc, hs, hw, block_input, cotangent, in_value, in_gate, out_proj, in_states, in_steps,
+        ndp, nz, sc, hs, hw, block_input, cotangent, in_value, in_gate, out_proj, in_states.T, in_steps.T,
         conv_value, conv_value_bias[None], gate_gain[None], heads_par, conv_states, conv_states_bias[None],
         norm_gain[None, :], lengths,
     )

time: 472 us -> 465 us (0.985)
    unnamed x48 -> x46, local copies, waits for them, and re-layouts: 11.3 us -> 8.36 us
where the time goes in v3:
time: 465 us; the launch traced here: 464 us
  Pallas kernels  401 us (86%)
  local copies, waits for them, and re-layouts  31.5 us (7%)
  other arithmetic  17.5 us (4%)
  starting transfers between devices  8.24 us (2%)
  waiting for transfers between devices  5.09 us (1%)
    pallas_call x1, Pallas kernels, gather_project(): pl.pallas_call(functools.partial(gather_kernel, ndp, nz, sc, hs, hw), in_...  153 us
    pallas_call x1, Pallas kernels, last_steps(): pl.pallas_call(functools.partial(last_kernel, ndp, nz, sc), in_specs=[any...  88 us
    pallas_call x1, Pallas kernels, conv_back(): pl.pallas_call(functools.partial(conv_back_kernel, nz, sc), in_specs=[any...  51.3 us
    pallas_call x1, Pallas kernels, unmix(): pl.pallas_call(functools.partial(unmix_kernel, ndp, nz, hs, hw, inner * 2...  44.4 us
    pallas_call x1, Pallas kernels, scan_backward(): pl.pallas_call(functools.partial(scan_bwd_kernel, places, inner // len(pl...  23.8 us
    pallas_call x1, Pallas kernels, mix(): pl.pallas_call(functools.partial(mix_kernel, ndp), grid=(nz,), in_specs=[...  16.3 us
    pallas_call x1, Pallas kernels, scan_forward(): pl.pallas_call(functools.partial(scan_fwd_kernel, places, inner // len(pl...  13.5 us
    pallas_call x1, Pallas kernels, weight_grad(): pl.pallas_call(functools.partial(weight_grad_kernel, ndp, 0 if sums is No...  10 us
  transfers between devices with their start and end apart: 9, of which 2 were waited for; matrix products, arithmetic and copies ran while one was open for 3% of the time, Pallas kernels for 26%

profile of v3, /device:TPU:0, one launch (start us, length us, event | category | flops | bytes accessed | tf_op | source)
XLA Modules:
  0.0 464.2 jit_solution(14631404438305624671)
XLA Ops:
  0.7 1.3 broadcast_in_dim.16.gain_ref
  2.0 1.2 broadcast_in_dim.13.cvb_ref
  4.4 1.3 pad_maximum_fusion.4.heads_ref
  5.7 153.5 %shard_map.288 = (bf16[4,4,384,384]{3,2,1,0:T(8,128)(2,1)}, bf16[4,4,80,384]{3,2,1,0:T(8,128)(2,1)}, bf16[4,4,384,384]{3,2,1,0:T(8,128)(2,1)}, bf16[4,4,384,384]...) custom-call(bf16[512,1536]{1,0:T(8,128)(2,1)} %x_hbm.1, ...), custom_call_target="tpu_custom_call" | custom-call | flops 11274289152 | bytes 62914560 | tf_op jit(solution)/shard_map/pallas_call | solution.py:707
  162.1 13.5 %shard_map.289 = (f32[1536,1024]{1,0:T(8,128)}, bf16[8,1536,128]{2,1,0:T(8,128)(2,1)S(1)}) custom-call(bf16[1536,1024]{1,0:T(8,128)(2,1)} %bitcast.68, f32[32,1024]{1,0:T(8,128)S(1)} %copy-done.13, f32[32,1024]{1,0:T(8,128)S(1)} %copy-done.16, f32[8,1152]{1,0:T(8,128)S(1)} %copy-done.17, bf16[1024,128]{1,0:T(8,128)(2,1)S(1)} %get-tuple-element.144.b_ref, ...), custom_call_target="tpu_custom_call" | custom-call | flops 4026531840 | bytes 15728640 | tf_op jit(solution)/shard_map/pallas_call | solution.py:192
  175.6 1.7 copy-done.10
  177.3 16.3 %shard_map.290 = (bf16[4,1024,384]{2,1,0:T(8,128)(2,1)S(1)}, f32[1536,1024]{1,0:T(8,128)}, f32[8,1024]{1,0:T(8,128)S(1)}) custom-call(bf16[4,4,384,384]{3,2,1,0:T(8,128)(2,1)} %get-tuple-element.82.wo_ref.wo_hbm, bf16[1536,1024]{1,0:T(8,128)(2,1)} %get-tuple-element.81.ct_ref.refs_0_, f32[1536,1024]{1,0:T(8,128)} %get-tuple-element.86.y_ref, ...), custom_call_target="tpu_custom_call" | custom-call | flops 4831838208 | bytes 34603008 | tf_op jit(solution)/shard_map/pallas_call | solution.py:827
  193.6 1.6 copy-done.7
  196.4 1.9 copy-done.2
  198.3 10.0 %shard_map.291 = bf16[4,4,384,384]{3,2,1,0:T(8,128)(2,1)} custom-call(bf16[1536,1024]{1,0:T(8,128)(2,1)S(1)} %copy-done.2, bf16[4,1024,384]{2,1,0:T(8,128)(2,1)} %copy-done.7, f32[8,1024]{1,0:T(8,128)S(1)} %add.97.refs_2_.sums_ref), custom_call_target="tpu_custom_call" | custom-call | flops 4831838208 | bytes 12582912 | tf_op jit(solution)/shard_map/pallas_call | solution.py:1039
  208.3 1.9 dynamic-slice_bitcast_fusion.2
  210.2 1.3 collective-permute-start.3
  212.4 44.4 %shard_map.292 = (bf16[1536,1024]{1,0:T(8,128)(2,1)}, bf16[4,1024,384]{2,1,0:T(8,128)(2,1)}, f32[4,8,384]{2,1,0:T(8,128)}, bf16[4,4,384,384]{3,2,1,0:T(8,128)(2,1)}, bf16[4,384,128]{2,1,0:T(8,128)(2,1)}) custom-call(f32[1536,1024]{1,0:T(8,128)} %get-tuple-element.86.y_ref, f32[1536,1024]{1,0:T(8,128)} %bitcast.74, f32[1536,1024]{1,0:T(8,128)} %get-tuple-element.87.h1_ref, ...), custom_call_target="tpu_custom_call" | custom-call | flops 5234491392 | bytes 44040192 | tf_op jit(solution)/shard_map/pallas_call | solution.py:974
  256.8 1.9 dynamic-slice_bitcast_fusion.1
  259.1 1.6 collective-permute-start.2
  260.8 1.6 fusion.6
  262.4 1.6 pad_maximum_fusion
  264.4 1.7 collective-permute-start.6
  266.1 23.8 %shard_map.293 = (f32[1536,1024]{1,0:T(8,128)}, f32[1024,128]{1,0:T(8,128)S(1)}, f32[1024,128]{1,0:T(8,128)S(1)}, f32[32,1024]{1,0:T(8,128)S(1)}, f32[32,1024]{1,0:T(8,128)S(1)}) custom-call(bf16[1536,1024]{1,0:T(8,128)(2,1)S(1)} %bitcast.70, bf16[1536,1024]{1,0:T(8,128)(2,1)} %get-tuple-element.94.dy_ref, f32[1536,1024]{1,0:T(8,128)} %get-tuple-element.86.y_ref, ...), custom_call_target="tpu_custom_call" | custom-call | flops 12079595520 | bytes 25165824 | tf_op jit(solution)/shard_map/pallas_call | solution.py:214
  289.9 2.0 fusion.5
  294.5 1.7 collective-permute-start.8
  296.8 3.9 collective-permute-done.5
  300.7 2.8 fusion.3.plane
  303.5 51.3 %shard_map.294 = (bf16[4,1024,384]{2,1,0:T(8,128)(2,1)}, bf16[1024,320]{1,0:T(8,128)(2,1)}, f32[4,16,384]{2,1,0:T(8,128)}, bf16[4,384,384]{2,1,0:T(8,128)(2,1)}) custom-call(f32[1536,1024]{1,0:T(8,128)} %get-tuple-element.98.dx_hbm, bf16[1536,1152]{1,0:T(8,128)(2,1)} %bitcast.85, f32[1024,128]{1,0:T(8,128)} %copy-done.11, f32[1024,128]{1,0:T(8,128)} %copy-done.12, ...), custom_call_target="tpu_custom_call" | custom-call | flops 4831838208 | bytes 41943040 | tf_op jit(solution)/shard_map/pallas_call | solution.py:1314
  354.8 3.5 fusion.1.plane
  358.2 88.0 %shard_map.295 = (f32[432,384]{1,0:T(8,128)}, bf16[512,1536]{1,0:T(8,128)(2,1)}, f32[8,1536]{1,0:T(8,128)}, f32[16,384]{1,0:T(8,128)}, bf16[512,1536]{1,0:T(8,128)(2,1)}, /*index=5*/bf16[4,384,384]{2,1,0:T(8,128)(2,1)}) custom-call(bf16[1536,1024]{1,0:T(8,128)(2,1)} %get-tuple-element.72.nt_ref.nt_hbm, bf16[4,1024,384]{2,1,0:T(8,128)(2,1)} %get-tuple-element.112.vl_hbm, ...), custom_call_target="tpu_custom_call" | custom-call | flops 9663676416 | bytes 41943040 | tf_op jit(solution)/shard_map/pallas_call | solution.py:1625
  449.0 2.0 slice.63
  451.0 1.4 slice_bitcast_fusion.3
  452.4 1.3 slice_bitcast_fusion.4
  453.7 1.4 slice_reduce_fusion.1
  455.1 1.3 slice.66
  458.1 1.4 slice_reduce_fusion
  (80 shorter events, 19.2 us)
Async XLA Ops:
  160.3 1.7 copy-start.9
  160.3 1.7 copy-start.13
  160.3 1.7 copy-start.16
  160.3 1.8 copy-start.17
  161.4 14.2 %copy-start.3 = (bf16[1024,128]{1,0:T(8,128)(2,1)}, bf16[1024,128]{1,0:T(8,128)(2,1)S(1)}, u32[]{:S(2)}) copy-start(bf16[1024,128]{1,0:T(8,128)(2,1)S(1)} %get-tuple-element.143.c_ref.cm_ref) | copy-start | bytes 786436
  162.0 15.3 %copy-start = (f32[1536,1]{1,0:T(8,128)}, f32[1536,1]{1,0:T(8,128)S(1)}, u32[]{:S(2)}) copy-start(f32[1536,1]{1,0:T(8,128)S(1)} %slice.78.gain_ref) | copy-start | bytes 18436
  175.6 1.7 copy-start.10
  193.6 1.6 copy-start.7
  195.2 1.2 collective-permute-start
  196.4 11.9 %copy-start.5 = (f32[8,1024]{1,0:T(8,128)}, f32[8,1024]{1,0:T(8,128)S(1)}, u32[]{:S(2)}) copy-start(f32[8,1024]{1,0:T(8,128)S(1)} %add.97.refs_2_.sums_ref) | copy-start | bytes 98308
  196.4 1.9 copy-start.2
  210.2 50.6 %collective-permute-start.3 = (bf16[4,192,384]{2,1,0:T(8,128)(2,1)S(1)}, bf16[4,192,384]{2,1,0:T(8,128)(2,1)S(1)}, u32[]{:S(2)}, u32[]{:S(2)}) collective-permute-start(bf16[4,192,384]{2,1,0:T(8,128)(2,1)S(1)} %get-tuple-element.91), channel_id=1, source_target_pairs={{0,8},{8,0},{16,24},{24,16},{1,9},{9,1},{17,25},{25,17},{2,10},{10... | collective-permute-start | bytes 1769480 | tf_op jit(solution)/shard_map/ppermute | solution.py:1687
  211.5 49.3 %collective-permute-start.4 = (bf16[4,192,384]{2,1,0:T(8,128)(2,1)S(1)}, bf16[4,192,384]{2,1,0:T(8,128)(2,1)S(1)}, u32[]{:S(2)}, u32[]{:S(2)}) collective-permute-start(bf16[4,192,384]{2,1,0:T(8,128)(2,1)S(1)} %get-tuple-element.92), channel_id=1, source_target_pairs={{0,16},{8,24},{16,0},{24,8},{1,17},{9,25},{17,1},{25,9},{2,18},{10... | collective-permute-start | bytes 1769480 | tf_op jit(solution)/shard_map/ppermute | solution.py:1692
  258.7 31.2 %collective-permute-start.1 = (bf16[4,192,384]{2,1,0:T(8,128)(2,1)S(1)}, bf16[4,192,384]{2,1,0:T(8,128)(2,1)S(1)}, u32[]{:S(2)}, u32[]{:S(2)}) collective-permute-start(bf16[4,192,384]{2,1,0:T(8,128)(2,1)S(1)} %get-tuple-element.136), channel_id=1, source_target_pairs={{0,8},{8,0},{16,24},{24,16},{1,9},{9,1},{17,25},{25,17},{2,10},{10... | collective-permute-start | bytes 1769480 | tf_op jit(solution)/shard_map/ppermute | solution.py:1687
  259.1 30.8 %collective-permute-start.2 = (bf16[4,192,384]{2,1,0:T(8,128)(2,1)S(1)}, bf16[4,192,384]{2,1,0:T(8,128)(2,1)S(1)}, u32[]{:S(2)}, u32[]{:S(2)}) collective-permute-start(bf16[4,192,384]{2,1,0:T(8,128)(2,1)S(1)} %get-tuple-element.135), channel_id=1, source_target_pairs={{0,16},{8,24},{16,0},{24,8},{1,17},{9,25},{17,1},{25,9},{2,18},{10... | collective-permute-start | bytes 1769480 | tf_op jit(solution)/shard_map/ppermute | solution.py:1692
  262.4 3.7 copy-start.1
  262.4 3.7 copy-start.4
  262.4 3.7 copy-start.8
  264.0 36.7 %collective-permute-start.5 = (bf16[4,384,384]{2,1,0:T(8,128)(2,1)}, bf16[4,384,384]{2,1,0:T(8,128)(2,1)S(1)}, u32[]{:S(2)}, u32[]{:S(2)}) collective-permute-start(bf16[4,384,384]{2,1,0:T(8,128)(2,1)} %get-tuple-element.103), channel_id=1, source_target_pairs={{0,16},{8,24},{16,0},{24,8},{1,17},{9,25},{17,1},{25,9},{2,18},{10... | collective-permute-start | bytes 3538952 | tf_op jit(solution)/shard_map/ppermute | solution.py:1692
  264.4 36.3 %collective-permute-start.6 = (bf16[4,384,384]{2,1,0:T(8,128)(2,1)}, bf16[4,384,384]{2,1,0:T(8,128)(2,1)S(1)}, u32[]{:S(2)}, u32[]{:S(2)}) collective-permute-start(bf16[4,384,384]{2,1,0:T(8,128)(2,1)} %get-tuple-element.104), channel_id=1, source_target_pairs={{0,8},{8,0},{16,24},{24,16},{1,9},{9,1},{17,25},{25,17},{2,10},{10... | collective-permute-start | bytes 3538952 | tf_op jit(solution)/shard_map/ppermute | solution.py:1687
  289.9 2.0 copy-start.11
  289.9 2.0 copy-start.12
  289.9 2.0 copy-start.14
  289.9 2.0 copy-start.15
  293.1 3.1 copy-start.6
  293.1 61.7 %collective-permute-start.7 = (bf16[4,384,384]{2,1,0:T(8,128)(2,1)}, bf16[4,384,384]{2,1,0:T(8,128)(2,1)}, u32[]{:S(2)}, u32[]{:S(2)}) collective-permute-start(bf16[4,384,384]{2,1,0:T(8,128)(2,1)} %pad_maximum_fusion.2), channel_id=1, source_target_pairs={{0,16},{8,24},{16,0},{24,8},{1,17},{9,25},{17,1},{25,9},{2,18},{10... | collective-permute-start | bytes 3538952 | tf_op jit(solution)/shard_map/ppermute | solution.py:1692
  294.5 60.2 %collective-permute-start.8 = (bf16[4,384,384]{2,1,0:T(8,128)(2,1)}, bf16[4,384,384]{2,1,0:T(8,128)(2,1)}, u32[]{:S(2)}, u32[]{:S(2)}) collective-permute-start(bf16[4,384,384]{2,1,0:T(8,128)(2,1)} %pad_maximum_fusion.3), channel_id=1, source_target_pairs={{0,8},{8,0},{16,24},{24,16},{1,9},{9,1},{17,25},{25,17},{2,10},{10... | collective-permute-start | bytes 3538952 | tf_op jit(solution)/shard_map/ppermute | solution.py:1687
  446.3 10.2 %copy-start.21 = (bf16[4,384,384]{2,1,0:T(8,128)(2,1)S(1)}, bf16[4,384,384]{2,1,0:T(8,128)(2,1)}, u32[]{:S(2)}) copy-start(bf16[4,384,384]{2,1,0:T(8,128)(2,1)} %get-tuple-element.124) | copy-start | bytes 3538948
  449.0 10.5 %copy-start.20 = (bf16[4,384,384]{2,1,0:T(8,128)(2,1)S(1)}, bf16[4,384,384]{2,1,0:T(8,128)(2,1)}, u32[]{:S(2)}) copy-start(bf16[4,384,384]{2,1,0:T(8,128)(2,1)} %get-tuple-element.127) | copy-start | bytes 3538948
  456.4 4.7 %copy-start.19 = (bf16[512,1536]{1,0:T(8,128)(2,1)S(1)}, bf16[512,1536]{1,0:T(8,128)(2,1)}, u32[]{:S(2)}) copy-start(bf16[512,1536]{1,0:T(8,128)(2,1)} %get-tuple-element.165) | copy-start | bytes 4718596
  461.1 2.0 copy-start.18
